TPU v7x, 32 devices: a whole 2x2x4 slice. The times are simulated.
32 devices in a mesh: dp: 8 (over z, y), seq: 4 (over x, core).
Axes of the slice: x: 2, y: 2, z: 4, core: 2. Of those that a mesh axis runs over, the one named last changes fastest.
Arguments:
- text_in: bfloat16 [8, 256, 768], P('dp', 'seq'), may hold values from -6 to 6
- image_in: bfloat16 [32, 196, 768], P('dp', 'seq'), may hold values from -6 to 6
- tile_slide: int32 [32], replicated, may hold values from 0 to 7, as said below
- owner_map: int32 [8], replicated, may hold values from 0 to 7, each once
- text_cot: bfloat16 [8, 256, 768], P('dp', 'seq'), may hold values from -6 to 6
- w_query: bfloat16 [768, 768], P(('dp', 'seq')), may hold values from -0.21875 to 0.21875
- w_key: bfloat16 [768, 768], P(('dp', 'seq')), may hold values from -0.21875 to 0.21875
- w_value: bfloat16 [768, 768], P(('dp', 'seq')), may hold values from -0.21875 to 0.21875
- w_out: bfloat16 [768, 768], P(('dp', 'seq')), may hold values from -0.875 to 0.875
- c_query: bfloat16 [768, 768], P(('dp', 'seq')), may hold values from -0.21875 to 0.21875
- c_key: bfloat16 [768, 768], P(('dp', 'seq')), may hold values from -0.21875 to 0.21875
- c_value: bfloat16 [768, 768], P(('dp', 'seq')), may hold values from -0.21875 to 0.21875
- c_out: bfloat16 [768, 768], P(('dp', 'seq')), may hold values from -3.5 to 3.5
- w_up: bfloat16 [768, 3072], P(('dp', 'seq')), may hold values from -0.21875 to 0.21875
- w_down: bfloat16 [3072, 768], P(('dp', 'seq')), may hold values from -0.109375 to 0.109375
- b_up: bfloat16 [3072], P(('dp', 'seq')), may hold values from -3 to 3
- b_down: bfloat16 [768], P(('dp', 'seq')), may hold values from -3 to 3
- self_gain: bfloat16 [768], P(('dp', 'seq')), may hold values from 0.5 to 1.5
- self_shift: bfloat16 [768], P(('dp', 'seq')), may hold values from -2 to 2
- cross_gain: bfloat16 [768], P(('dp', 'seq')), may hold values from 0.5 to 1.5
- cross_shift: bfloat16 [768], P(('dp', 'seq')), may hold values from -2 to 2
- tile_gain: bfloat16 [768], P(('dp', 'seq')), may hold values from 0.5 to 1.5
- tile_shift: bfloat16 [768], P(('dp', 'seq')), may hold values from -2 to 2
- mlp_gain: bfloat16 [768], P(('dp', 'seq')), may hold values from 0.5 to 1.5
- mlp_shift: bfloat16 [768], P(('dp', 'seq')), may hold values from -2 to 2
Outputs:
- text_out: bfloat16 [8, 256, 768], P('dp', 'seq')
- text_grad: bfloat16 [8, 256, 768], P('dp', 'seq')
- image_grad: bfloat16 [32, 196, 768], P('dp', 'seq')
- query_grad: float32 [768, 768], P(('dp', 'seq'))
- key_grad: float32 [768, 768], P(('dp', 'seq'))
- value_grad: float32 [768, 768], P(('dp', 'seq'))
- proj_grad: float32 [768, 768], P(('dp', 'seq'))
- xquery_grad: float32 [768, 768], P(('dp', 'seq'))
- xkey_grad: float32 [768, 768], P(('dp', 'seq'))
- xvalue_grad: float32 [768, 768], P(('dp', 'seq'))
- xproj_grad: float32 [768, 768], P(('dp', 'seq'))
- up_grad: float32 [768, 3072], P(('dp', 'seq'))
- down_grad: float32 [3072, 768], P(('dp', 'seq'))
- upbias_grad: float32 [3072], P(('dp', 'seq'))
- downbias_grad: float32 [768], P(('dp', 'seq'))
- sgain_grad: float32 [768], P(('dp', 'seq'))
- sshift_grad: float32 [768], P(('dp', 'seq'))
- xgain_grad: float32 [768], P(('dp', 'seq'))
- xshift_grad: float32 [768], P(('dp', 'seq'))
- tgain_grad: float32 [768], P(('dp', 'seq'))
- tshift_grad: float32 [768], P(('dp', 'seq'))
- mgain_grad: float32 [768], P(('dp', 'seq'))
- mshift_grad: float32 [768], P(('dp', 'seq'))
Inputs may be any that keep to these rules, and one draw needn't show every extreme that they name: `tile_slide`: no index of dp holds two tiles of the same slide; every slide has one tile or more; some slide has a tile on every index of dp. A permutation: row c of text_in, text_cot and text_out is the caption of the slide s with owner_map[s] = c.
All inputs are finite; a program needn't handle non-finite values.
Results may differ from a plain program's by a relative error of at most 0.024.
Values may be sent and summed in bfloat16 or wider, within the bound.
A program may use at most 256 MiB of HBM per device.

v0:
```python
from functools import partial
import math

import jax
import jax.numpy as jnp
from jax import lax
from jax.sharding import PartitionSpec as P

HEAD = 64


EPSILON = 1e-05
MASKED_SCORE = -1e30


def combined_all(x, axis, combine):
    everything = jax.tree.map(lambda part: lax.all_gather(part, axis), x)
    initial = jax.tree.map(lambda part: part[0], everything)

    def step(k, so_far):
        return combine(so_far, jax.tree.map(lambda part: part[k], everything))

    return lax.fori_loop(1, lax.axis_size(axis), step, initial)


def norm_rows(values, gain_row, shift_row):
    average = jnp.mean(values, axis=-1, keepdims=True)
    centered = values - average
    spread = jnp.mean(centered * centered, axis=-1, keepdims=True)
    return centered * lax.rsqrt(spread + EPSILON) * gain_row + shift_row


def matmul(former, latter):
    return jnp.dot(former, latter, preferred_element_type=jnp.float32)


def matmul_trans(former, latter):
    return lax.dot_general(
        former, latter, (((1,), (1,)), ((), ())), preferred_element_type=jnp.float32
    )


def outer_sum(former, latter):
    return lax.dot_general(
        former, latter, (((0,), (0,)), ((), ())), preferred_element_type=jnp.float32
    )


def head_pair(matrix, pair_index):
    columns = lax.dynamic_slice_in_dim(matrix, pair_index * 2 * HEAD, 2 * HEAD, 1)
    return columns.reshape(columns.shape[0], 2, HEAD)


def put_pair(matrix, update, pair_index):
    return lax.dynamic_update_slice_in_dim(
        matrix, update.reshape(update.shape[0], 2 * HEAD), pair_index * 2 * HEAD, 1
    )


def pick_pair(stacked, pair_index):
    return lax.dynamic_index_in_dim(stacked, pair_index, 0, keepdims=False)


def pair_scores(query_rows, key_rows, allowed, pair_index):
    factor = 1.0 / math.sqrt(HEAD)
    scores = (
        jnp.einsum(
            "qhd,khd->hqk",
            head_pair(query_rows, pair_index),
            head_pair(key_rows, pair_index),
            preferred_element_type=jnp.float32,
        )
        * factor
    )
    return jnp.where(allowed[None], scores, MASKED_SCORE)


def attend_stats(query_rows, key_rows, allowed):
    pair_count = query_rows.shape[1] // (2 * HEAD)

    def one_pair(pair_index, state_now):
        row_max, row_sum = state_now
        scores = pair_scores(query_rows, key_rows, allowed, pair_index)
        highest = jnp.max(scores, axis=2)
        summed = jnp.sum(jnp.exp(scores - highest[..., None]), axis=2)
        return (
            lax.dynamic_update_index_in_dim(row_max, highest, pair_index, 0),
            lax.dynamic_update_index_in_dim(row_sum, summed, pair_index, 0),
        )

    empty_stats = jnp.zeros((pair_count, 2, query_rows.shape[0]), jnp.float32)
    return lax.fori_loop(0, pair_count, one_pair, (empty_stats, empty_stats))


def attend_forward(query_rows, key_rows, value_rows, allowed, maxima, totals):
    pair_count = query_rows.shape[1] // (2 * HEAD)
    stats_given = maxima is not None
    if not stats_given:
        maxima = jnp.zeros((pair_count, 2, query_rows.shape[0]), jnp.float32)
        totals = jnp.zeros_like(maxima)

    def one_pair(pair_index, state_now):
        output, row_max, row_sum = state_now
        scores = pair_scores(query_rows, key_rows, allowed, pair_index)
        if stats_given:
            highest = pick_pair(row_max, pair_index)
            exponent = jnp.exp(scores - highest[..., None])
            summed = pick_pair(row_sum, pair_index)
        else:
            highest = jnp.max(scores, axis=2)
            exponent = jnp.exp(scores - highest[..., None])
            summed = jnp.sum(exponent, axis=2)
            row_max = lax.dynamic_update_index_in_dim(row_max, highest, pair_index, 0)
            row_sum = lax.dynamic_update_index_in_dim(row_sum, summed, pair_index, 0)
        weights = (exponent / summed[..., None]).astype(jnp.bfloat16)
        mixture = jnp.einsum(
            "hqk,khd->qhd",
            weights,
            head_pair(value_rows, pair_index),
            preferred_element_type=jnp.float32,
        )
        return (put_pair(output, mixture, pair_index), row_max, row_sum)

    start_state = (jnp.zeros(query_rows.shape, jnp.float32), maxima, totals)
    return lax.fori_loop(0, pair_count, one_pair, start_state)


def attend_rowsums(query_rows, key_rows, value_rows, allowed, maxima, totals, grad_rows):
    pair_count = query_rows.shape[1] // (2 * HEAD)

    def one_pair(pair_index, row_terms):
        scores = pair_scores(query_rows, key_rows, allowed, pair_index)
        chances = (
            jnp.exp(scores - pick_pair(maxima, pair_index)[..., None])
            / pick_pair(totals, pair_index)[..., None]
        )
        grad_chances = jnp.einsum(
            "qhd,khd->hqk",
            head_pair(grad_rows, pair_index),
            head_pair(value_rows, pair_index),
            preferred_element_type=jnp.float32,
        )
        return lax.dynamic_update_index_in_dim(
            row_terms, jnp.sum(chances * grad_chances, axis=2), pair_index, 0
        )

    return lax.fori_loop(0, pair_count, one_pair, jnp.zeros_like(maxima))


def attend_backward(
    query_rows, key_rows, value_rows, allowed, maxima, totals, grad_rows, row_terms
):
    pair_count = query_rows.shape[1] // (2 * HEAD)
    factor = 1.0 / math.sqrt(HEAD)

    def one_pair(pair_index, state_now):
        grad_query, grad_key, grad_value = state_now
        scores = pair_scores(query_rows, key_rows, allowed, pair_index)
        chances = (
            jnp.exp(scores - pick_pair(maxima, pair_index)[..., None])
            / pick_pair(totals, pair_index)[..., None]
        )
        grad_heads = head_pair(grad_rows, pair_index)
        grad_chances = jnp.einsum(
            "qhd,khd->hqk",
            grad_heads,
            head_pair(value_rows, pair_index),
            preferred_element_type=jnp.float32,
        )
        if row_terms is None:
            weighted = jnp.sum(chances * grad_chances, axis=2)
        else:
            weighted = pick_pair(row_terms, pair_index)
        grad_scores = (chances * (grad_chances - weighted[..., None])).astype(jnp.bfloat16)
        query_part = (
            jnp.einsum(
                "hqk,khd->qhd",
                grad_scores,
                head_pair(key_rows, pair_index),
                preferred_element_type=jnp.float32,
            )
            * factor
        )
        key_part = (
            jnp.einsum(
                "hqk,qhd->khd",
                grad_scores,
                head_pair(query_rows, pair_index),
                preferred_element_type=jnp.float32,
            )
            * factor
        )
        value_part = jnp.einsum(
            "hqk,qhd->khd",
            chances.astype(jnp.bfloat16),
            grad_heads,
            preferred_element_type=jnp.float32,
        )
        return (
            put_pair(grad_query, query_part, pair_index),
            put_pair(grad_key, key_part, pair_index),
            put_pair(grad_value, value_part, pair_index),
        )

    start_state = (
        jnp.zeros(query_rows.shape, jnp.float32),
        jnp.zeros(key_rows.shape, jnp.float32),
        jnp.zeros(value_rows.shape, jnp.float32),
    )
    return lax.fori_loop(0, pair_count, one_pair, start_state)


def join_stats(former, latter):
    highest = jnp.maximum(former[0], latter[0])
    return (
        highest,
        former[1] * jnp.exp(former[0] - highest) + latter[1] * jnp.exp(latter[0] - highest),
    )


def split_rows(matrix, data_count, seq_count):
    return matrix.reshape(
        data_count, seq_count, matrix.shape[0] // (data_count * seq_count), matrix.shape[1]
    )


def fold_rows(pieces):
    return jnp.sum(pieces, axis=1).reshape(pieces.shape[0] * pieces.shape[2], pieces.shape[3])


def per_device(
    text_in,
    image_in,
    tile_slide,
    owner_map,
    text_cot,
    w_query,
    w_key,
    w_value,
    w_out,
    c_query,
    c_key,
    c_value,
    c_out,
    w_up,
    w_down,
    b_up,
    b_down,
    self_gain,
    self_shift,
    cross_gain,
    cross_shift,
    tile_gain,
    tile_shift,
    mlp_gain,
    mlp_shift,
):
    gathered = (
        lax.all_gather(w_query, ("dp", "seq"), axis=0, tiled=True),
        lax.all_gather(w_key, ("dp", "seq"), axis=0, tiled=True),
        lax.all_gather(w_value, ("dp", "seq"), axis=0, tiled=True),
        lax.all_gather(w_out, ("dp", "seq"), axis=0, tiled=True),
        lax.all_gather(c_query, ("dp", "seq"), axis=0, tiled=True),
        lax.all_gather(c_key, ("dp", "seq"), axis=0, tiled=True),
        lax.all_gather(c_value, ("dp", "seq"), axis=0, tiled=True),
        lax.all_gather(c_out, ("dp", "seq"), axis=0, tiled=True),
        lax.all_gather(w_up, ("dp", "seq"), axis=0, tiled=True),
        lax.all_gather(w_down, ("dp", "seq"), axis=0, tiled=True),
        lax.all_gather(b_up, ("dp", "seq"), axis=0, tiled=True),
        lax.all_gather(b_down, ("dp", "seq"), axis=0, tiled=True),
        lax.all_gather(self_gain, ("dp", "seq"), axis=0, tiled=True),
        lax.all_gather(self_shift, ("dp", "seq"), axis=0, tiled=True),
        lax.all_gather(cross_gain, ("dp", "seq"), axis=0, tiled=True),
        lax.all_gather(cross_shift, ("dp", "seq"), axis=0, tiled=True),
        lax.all_gather(tile_gain, ("dp", "seq"), axis=0, tiled=True),
        lax.all_gather(tile_shift, ("dp", "seq"), axis=0, tiled=True),
        lax.all_gather(mlp_gain, ("dp", "seq"), axis=0, tiled=True),
        lax.all_gather(mlp_shift, ("dp", "seq"), axis=0, tiled=True),
    )
    query_mat, key_mat, value_mat, proj_mat = (gathered[0], gathered[1], gathered[2], gathered[3])
    xquery_mat, xkey_mat, xvalue_mat, xproj_mat = (
        gathered[4],
        gathered[5],
        gathered[6],
        gathered[7],
    )
    up_mat, down_mat = (gathered[8], gathered[9])
    vectors = [member.astype(jnp.float32) for member in gathered[10:]]
    (
        up_bias,
        down_bias,
        gain_one,
        shift_one,
        gain_two,
        shift_two,
        gain_tile,
        shift_tile,
        gain_three,
        shift_three,
    ) = vectors
    text_rows = text_in[0].astype(jnp.float32)
    rows_here = text_rows.shape[0]
    hidden_dim = text_rows.shape[1]
    normed_one, norm_one_back = jax.vjp(norm_rows, text_rows, gain_one, shift_one)
    first_in = normed_one.astype(jnp.bfloat16)
    query_one = matmul(first_in, query_mat).astype(jnp.bfloat16)
    key_one = matmul(first_in, key_mat).astype(jnp.bfloat16)
    value_one = matmul(first_in, value_mat).astype(jnp.bfloat16)
    key_all, value_all = (
        lax.all_gather(key_one, "seq", axis=0, tiled=True),
        lax.all_gather(value_one, "seq", axis=0, tiled=True),
    )
    positions = lax.axis_index("seq") * rows_here + jnp.arange(rows_here)
    causal = positions[:, None] >= jnp.arange(key_all.shape[0])[None, :]
    attend_one, max_one, sum_one = attend_forward(query_one, key_all, value_all, causal, None, None)
    mixed_one = attend_one.astype(jnp.bfloat16)
    second = text_rows + matmul(mixed_one, proj_mat)
    normed_two, norm_two_back = jax.vjp(norm_rows, second, gain_two, shift_two)
    second_in = normed_two.astype(jnp.bfloat16)
    query_two = matmul(second_in, xquery_mat).astype(jnp.bfloat16)
    tile_rows = image_in.astype(jnp.float32)
    normed_tiles, norm_tile_back = jax.vjp(norm_rows, tile_rows, gain_tile, shift_tile)
    tiles_in = normed_tiles.astype(jnp.bfloat16)
    data_index = lax.axis_index("dp")
    data_count = lax.axis_size("dp")
    seq_count = lax.axis_size("seq")
    tile_count = image_in.shape[0]
    slot_rows = image_in.shape[1]
    slide_ids = jnp.arange(owner_map.shape[0])
    destination = jnp.sum(
        jnp.where(tile_slide[:, None] == slide_ids[None, :], owner_map[None, :], 0), axis=1
    )
    own_destination = lax.dynamic_slice_in_dim(destination, data_index * tile_count, tile_count)
    routing = (own_destination[None, :] == jnp.arange(data_count)[:, None]).astype(jnp.bfloat16)
    outgoing = jnp.einsum(
        "pt,trd->prd", routing, tiles_in, preferred_element_type=jnp.float32
    ).astype(jnp.bfloat16)
    incoming = lax.all_to_all(outgoing, "dp", split_axis=0, concat_axis=0, tiled=True)
    arrived = jnp.any(destination.reshape(data_count, tile_count) == data_index, axis=1)
    flat_in = incoming.reshape(data_count * slot_rows, hidden_dim)
    allowed_rows = jnp.broadcast_to(arrived[:, None], (data_count, slot_rows)).reshape(-1)
    key_two = matmul(flat_in, xkey_mat).astype(jnp.bfloat16)
    value_two = matmul(flat_in, xvalue_mat).astype(jnp.bfloat16)
    query_far = lax.all_gather(query_two, "seq", axis=0, tiled=True)
    allowed_near = allowed_rows[None, :]
    local_max, local_sum = attend_stats(query_far, key_two, allowed_near)
    max_two, sum_two = combined_all((local_max, local_sum), "seq", join_stats)
    partial_rows = attend_forward(query_far, key_two, value_two, allowed_near, max_two, sum_two)[0]
    attend_two = lax.psum_scatter(
        partial_rows.astype(jnp.bfloat16), "seq", scatter_dimension=0, tiled=True
    )
    third_sum = second + matmul(attend_two, xproj_mat)
    normed_three, norm_three_back = jax.vjp(norm_rows, third_sum, gain_three, shift_three)
    third_in = normed_three.astype(jnp.bfloat16)
    pre_gelu = matmul(third_in, up_mat) + up_bias
    activated, gelu_back = jax.vjp(partial(jax.nn.gelu, approximate=False), pre_gelu)
    act_in = activated.astype(jnp.bfloat16)
    result = third_sum + matmul(act_in, down_mat) + down_bias
    text_out = result.astype(jnp.bfloat16)[None]
    cot_rows = text_cot[0]
    grad_res = cot_rows.astype(jnp.float32)
    down_grad = outer_sum(act_in, cot_rows)
    downbias_grad = jnp.sum(grad_res, axis=0)
    grad_act = matmul_trans(cot_rows, down_mat).astype(jnp.bfloat16)
    grad_pre = gelu_back(grad_act.astype(jnp.float32))[0].astype(jnp.bfloat16)
    up_grad = outer_sum(third_in, grad_pre)
    upbias_grad = jnp.sum(grad_pre.astype(jnp.float32), axis=0)
    grad_mid, mgain_grad, mshift_grad = norm_three_back(matmul_trans(grad_pre, up_mat))
    grad_third = grad_res + grad_mid
    branch_two = grad_third.astype(jnp.bfloat16)
    xproj_grad = outer_sum(attend_two, branch_two)
    grad_attend_two = matmul_trans(branch_two, xproj_mat).astype(jnp.bfloat16)
    grad_far = lax.all_gather(grad_attend_two, "seq", axis=0, tiled=True)
    row_part = attend_rowsums(
        query_far, key_two, value_two, allowed_near, max_two, sum_two, grad_far
    )
    row_terms = lax.psum(row_part, "seq")
    query_grad_far, key_grad_two, value_grad_two = attend_backward(
        query_far, key_two, value_two, allowed_near, max_two, sum_two, grad_far, row_terms
    )
    query_grad_two = lax.psum_scatter(
        query_grad_far.astype(jnp.bfloat16), "seq", scatter_dimension=0, tiled=True
    )
    gkey_two = key_grad_two.astype(jnp.bfloat16)
    gvalue_two = value_grad_two.astype(jnp.bfloat16)
    xquery_grad = outer_sum(second_in, query_grad_two)
    xkey_grad = outer_sum(flat_in, gkey_two)
    xvalue_grad = outer_sum(flat_in, gvalue_two)
    grad_flat = (matmul_trans(gkey_two, xkey_mat) + matmul_trans(gvalue_two, xvalue_mat)).astype(
        jnp.bfloat16
    )
    grad_home = lax.all_to_all(
        grad_flat.reshape(data_count, slot_rows, hidden_dim),
        "dp",
        split_axis=0,
        concat_axis=0,
        tiled=True,
    )
    grad_tiles = jnp.einsum("pt,prd->trd", routing, grad_home, preferred_element_type=jnp.float32)
    image_back, tgain_grad, tshift_grad = norm_tile_back(grad_tiles)
    image_grad = image_back.astype(jnp.bfloat16)
    grad_mid_two, xgain_grad, xshift_grad = norm_two_back(matmul_trans(query_grad_two, xquery_mat))
    grad_second = grad_third + grad_mid_two
    branch_one = grad_second.astype(jnp.bfloat16)
    proj_grad = outer_sum(mixed_one, branch_one)
    grad_attend_one = matmul_trans(branch_one, proj_mat).astype(jnp.bfloat16)
    query_grad_one, key_grad_all, value_grad_all = attend_backward(
        query_one, key_all, value_all, causal, max_one, sum_one, grad_attend_one, None
    )
    key_grad_one, value_grad_one = (
        lax.psum_scatter(
            key_grad_all.astype(jnp.bfloat16), "seq", scatter_dimension=0, tiled=True
        ).astype(jnp.float32),
        lax.psum_scatter(
            value_grad_all.astype(jnp.bfloat16), "seq", scatter_dimension=0, tiled=True
        ).astype(jnp.float32),
    )
    gquery_one = query_grad_one.astype(jnp.bfloat16)
    gkey_one = key_grad_one.astype(jnp.bfloat16)
    gvalue_one = value_grad_one.astype(jnp.bfloat16)
    query_grad = outer_sum(first_in, gquery_one)
    key_grad = outer_sum(first_in, gkey_one)
    value_grad = outer_sum(first_in, gvalue_one)
    grad_norm_one = (
        matmul_trans(gquery_one, query_mat)
        + matmul_trans(gkey_one, key_mat)
        + matmul_trans(gvalue_one, value_mat)
    )
    grad_mid_one, sgain_grad, sshift_grad = norm_one_back(grad_norm_one)
    text_grad = (grad_second + grad_mid_one).astype(jnp.bfloat16)[None]
    pieces = (
        lax.all_to_all(
            split_rows(query_grad, data_count, seq_count).astype(jnp.bfloat16),
            "seq",
            split_axis=1,
            concat_axis=1,
            tiled=True,
        ).astype(jnp.float32),
        lax.all_to_all(
            split_rows(key_grad, data_count, seq_count).astype(jnp.bfloat16),
            "seq",
            split_axis=1,
            concat_axis=1,
            tiled=True,
        ).astype(jnp.float32),
        lax.all_to_all(
            split_rows(value_grad, data_count, seq_count).astype(jnp.bfloat16),
            "seq",
            split_axis=1,
            concat_axis=1,
            tiled=True,
        ).astype(jnp.float32),
        lax.all_to_all(
            split_rows(proj_grad, data_count, seq_count).astype(jnp.bfloat16),
            "seq",
            split_axis=1,
            concat_axis=1,
            tiled=True,
        ).astype(jnp.float32),
        lax.all_to_all(
            split_rows(xquery_grad, data_count, seq_count).astype(jnp.bfloat16),
            "seq",
            split_axis=1,
            concat_axis=1,
            tiled=True,
        ).astype(jnp.float32),
        lax.all_to_all(
            split_rows(xkey_grad, data_count, seq_count).astype(jnp.bfloat16),
            "seq",
            split_axis=1,
            concat_axis=1,
            tiled=True,
        ).astype(jnp.float32),
        lax.all_to_all(
            split_rows(xvalue_grad, data_count, seq_count).astype(jnp.bfloat16),
            "seq",
            split_axis=1,
            concat_axis=1,
            tiled=True,
        ).astype(jnp.float32),
        lax.all_to_all(
            split_rows(xproj_grad, data_count, seq_count).astype(jnp.bfloat16),
            "seq",
            split_axis=1,
            concat_axis=1,
            tiled=True,
        ).astype(jnp.float32),
        lax.all_to_all(
            split_rows(up_grad, data_count, seq_count).astype(jnp.bfloat16),
            "seq",
            split_axis=1,
            concat_axis=1,
            tiled=True,
        ).astype(jnp.float32),
        lax.all_to_all(
            split_rows(down_grad, data_count, seq_count).astype(jnp.bfloat16),
            "seq",
            split_axis=1,
            concat_axis=1,
            tiled=True,
        ).astype(jnp.float32),
    )
    folded = [fold_rows(member) for member in pieces]
    summed_mats = (
        lax.psum_scatter(folded[0], "dp", scatter_dimension=0, tiled=True),
        lax.psum_scatter(folded[1], "dp", scatter_dimension=0, tiled=True),
        lax.psum_scatter(folded[2], "dp", scatter_dimension=0, tiled=True),
        lax.psum_scatter(folded[3], "dp", scatter_dimension=0, tiled=True),
        lax.psum_scatter(folded[4], "dp", scatter_dimension=0, tiled=True),
        lax.psum_scatter(folded[5], "dp", scatter_dimension=0, tiled=True),
        lax.psum_scatter(folded[6], "dp", scatter_dimension=0, tiled=True),
        lax.psum_scatter(folded[7], "dp", scatter_dimension=0, tiled=True),
        lax.psum_scatter(folded[8], "dp", scatter_dimension=0, tiled=True),
        lax.psum_scatter(folded[9], "dp", scatter_dimension=0, tiled=True),
    )
    summed_vecs = (
        lax.psum_scatter(upbias_grad, ("dp", "seq"), scatter_dimension=0, tiled=True),
        lax.psum_scatter(downbias_grad, ("dp", "seq"), scatter_dimension=0, tiled=True),
        lax.psum_scatter(sgain_grad, ("dp", "seq"), scatter_dimension=0, tiled=True),
        lax.psum_scatter(sshift_grad, ("dp", "seq"), scatter_dimension=0, tiled=True),
        lax.psum_scatter(xgain_grad, ("dp", "seq"), scatter_dimension=0, tiled=True),
        lax.psum_scatter(xshift_grad, ("dp", "seq"), scatter_dimension=0, tiled=True),
        lax.psum_scatter(tgain_grad, ("dp", "seq"), scatter_dimension=0, tiled=True),
        lax.psum_scatter(tshift_grad, ("dp", "seq"), scatter_dimension=0, tiled=True),
        lax.psum_scatter(mgain_grad, ("dp", "seq"), scatter_dimension=0, tiled=True),
        lax.psum_scatter(mshift_grad, ("dp", "seq"), scatter_dimension=0, tiled=True),
    )
    return (text_out, text_grad, image_grad) + tuple(summed_mats) + tuple(summed_vecs)


def solution(mesh):
    placed = (
        P("dp", "seq", None),
        P("dp", "seq", None),
        P(),
        P(),
        P("dp", "seq", None),
        P(("dp", "seq"), None),
        P(("dp", "seq"), None),
        P(("dp", "seq"), None),
        P(("dp", "seq"), None),
        P(("dp", "seq"), None),
        P(("dp", "seq"), None),
        P(("dp", "seq"), None),
        P(("dp", "seq"), None),
        P(("dp", "seq"), None),
        P(("dp", "seq"), None),
        P(("dp", "seq")),
        P(("dp", "seq")),
        P(("dp", "seq")),
        P(("dp", "seq")),
        P(("dp", "seq")),
        P(("dp", "seq")),
        P(("dp", "seq")),
        P(("dp", "seq")),
        P(("dp", "seq")),
        P(("dp", "seq")),
    )
    return jax.shard_map(
        per_device,
        mesh=mesh,
        in_specs=placed,
        out_specs=(
            P("dp", "seq", None),
            P("dp", "seq", None),
            P("dp", "seq", None),
            P(("dp", "seq"), None),
            P(("dp", "seq"), None),
            P(("dp", "seq"), None),
            P(("dp", "seq"), None),
            P(("dp", "seq"), None),
            P(("dp", "seq"), None),
            P(("dp", "seq"), None),
            P(("dp", "seq"), None),
            P(("dp", "seq"), None),
            P(("dp", "seq"), None),
            P(("dp", "seq")),
            P(("dp", "seq")),
            P(("dp", "seq")),
            P(("dp", "seq")),
            P(("dp", "seq")),
            P(("dp", "seq")),
            P(("dp", "seq")),
            P(("dp", "seq")),
            P(("dp", "seq")),
            P(("dp", "seq")),
        ),
        check_vma=False,
    )
```

profile of v0, /device:TPU:0, one launch (start us, length us, event | category | flops | bytes accessed | tf_op | source)
XLA Modules:
  0.0 1493.1 jit_solution(4504398638059074348)
XLA Ops:
  20.3 42.7 %all-reduce.21 = (bf16[768]{0:T(1024)(128)(2,1)S(1)}, bf16[768]{0:T(1024)(128)(2,1)S(1)}, bf16[768]{0:T(1024)(128)(2,1)S(1)}, bf16[768]{0:T(1024)(128)(2,1)S(1)}...) all-reduce(bf16[768]{0:T(1024)(128)(2,1)S(1)} %dynamic-update-slice, ...), channel_id=1, replica_groups=mesh['dp'=8,'seq'=4] {'dp','seq'}, use_global_device_ids=true, to_apply=%add.1 | all-reduce | flops 9984 | bytes 39936
  69.1 5.1 all-to-all-start
  75.7 15.8 %all-to-all-done = bf16[8,49,768]{2,1,0:T(8,128)(2,1)S(1)} async-done(((bf16[8,49,768]{2,1,0:T(8,128)(2,1)}), bf16[8,49,768]{2,1,0:T(8,128)(2,1)S(1)}, u32[]{:S(2)}, u32[]{:S(2)}) %all-to-all-start) | async-done | bytes 602144 | tf_op jit(solution)/shard_map/all_to_all | solution.py:338
  93.6 7.5 all_gather.87
  101.3 23.6 %all-gather.17.cloned.1.call-done = bf16[768,768]{1,0:T(8,128)(2,1)} async-done(((bf16[24,768]{1,0:T(8,128)(2,1)}), bf16[768,768]{1,0:T(8,128)(2,1)}) %all-gather.17.cloned.1.call-update) | async-done | bytes 1179664 | tf_op jit(solution)/shard_map/all_gather | solution.py:260
  126.5 6.5 all_gather.90
  133.2 47.6 %all-gather.15.cloned.1.call-done = bf16[768,768]{1,0:T(8,128)(2,1)} async-done(((bf16[24,768]{1,0:T(8,128)(2,1)}), bf16[768,768]{1,0:T(8,128)(2,1)}) %all-gather.15.cloned.1.call-update) | async-done | bytes 1179664 | tf_op jit(solution)/shard_map/all_gather | solution.py:259
  182.5 8.9 while.128
  191.5 45.1 %all-gather.19.cloned.1.call-done = bf16[768,768]{1,0:T(8,128)(2,1)} async-done(((bf16[24,768]{1,0:T(8,128)(2,1)}), bf16[768,768]{1,0:T(8,128)(2,1)}) %all-gather.19.cloned.1.call-update) | async-done | bytes 1179664 | tf_op jit(solution)/shard_map/all_gather | solution.py:262
  238.6 53.8 %all-gather.23.cloned.1.call-done = bf16[768,768]{1,0:T(8,128)(2,1)} async-done(((bf16[24,768]{1,0:T(8,128)(2,1)}), bf16[768,768]{1,0:T(8,128)(2,1)}) %all-gather.23.cloned.1.call-update) | async-done | bytes 1179664 | tf_op jit(solution)/shard_map/all_gather | solution.py:263
  294.1 6.5 all_gather.98
  300.7 47.4 %all-gather.25.cloned.1.call-done = bf16[768,768]{1,0:T(8,128)(2,1)} async-done(((bf16[24,768]{1,0:T(8,128)(2,1)}), bf16[768,768]{1,0:T(8,128)(2,1)}) %all-gather.25.cloned.1.call-update) | async-done | bytes 1179664 | tf_op jit(solution)/shard_map/all_gather | solution.py:264
  350.3 4.3 while.129
  354.7 5.2 all-gather
  359.9 5.2 all-gather.1
  365.3 38.7 %all-gather.21.cloned.1.call-done = bf16[768,768]{1,0:T(8,128)(2,1)} async-done(((bf16[24,768]{1,0:T(8,128)(2,1)}), bf16[768,768]{1,0:T(8,128)(2,1)}) %all-gather.21.cloned.1.call-update) | async-done | bytes 1179664 | tf_op jit(solution)/shard_map/all_gather | solution.py:265
  404.0 2.8 convolution_convert_fusion.12
  408.1 5.0 while.130
  415.7 44.2 %all-gather.27.cloned.1.call-done = bf16[768,768]{1,0:T(8,128)(2,1)} async-done(((bf16[24,768]{1,0:T(8,128)(2,1)}), bf16[768,768]{1,0:T(8,128)(2,1)}) %all-gather.27.cloned.1.call-update) | async-done | bytes 1179664 | tf_op jit(solution)/shard_map/all_gather | solution.py:266
  459.9 22.3 %reduce-scatter.43.cloned.1.call-done = bf16[64,768]{1,0:T(8,128)(2,1)} async-done(((bf16[256,768]{1,0:T(8,128)(2,1)}), bf16[64,768]{1,0:T(8,128)(2,1)}) %reduce-scatter.43.cloned.1.call-update) | async-done | bytes 98320
  484.2 64.4 %all-gather.29.cloned.1.call-done = bf16[768,3072]{1,0:T(8,128)(2,1)} async-done(((bf16[24,3072]{1,0:T(8,128)(2,1)}), bf16[768,3072]{1,0:T(8,128)(2,1)}) %all-gather.29.cloned.1.call-update) | async-done | bytes 4718608 | tf_op jit(solution)/shard_map/all_gather | solution.py:267
  548.6 5.8 fusion.65
  554.4 59.6 %all-gather.31.cloned.1.call-done = bf16[3072,768]{1,0:T(8,128)(2,1)} async-done(((bf16[96,768]{1,0:T(8,128)(2,1)}), bf16[3072,768]{1,0:T(8,128)(2,1)}) %all-gather.31.cloned.1.call-update) | async-done | bytes 4718608 | tf_op jit(solution)/shard_map/all_gather | solution.py:268
  614.0 5.9 convert_reduce_fusion.10
  623.8 6.9 all_gather.111
  632.5 35.5 %while.131 = (s32[]{:T(128)}, f32[6,2,256]{2,1,0:T(2,128)}, bf16[256,768]{0,1:T(8,128)(2,1)S(1)}, bf16[392,768]{0,1:T(8,128)(2,1)S(1)}, f32[6,2,256]{2,1,0:T(2,1...) while((s32[]{:T(128)}, f32[6,2,256]{2,1,0:T(2,128)}, ...), condition=%wide.region_27.28_spmd.clone, body=%wide.region_25.27_spmd.clone.sunk | while | flops 52583940 | bytes 2621663 | solution.py:147
  668.0 12.1 psum.7
  682.8 26.4 %while.132 = (s32[]{:T(128)}, bf16[256,768]{0,1:T(8,128)(2,1)}, bf16[392,768]{0,1:T(8,128)(2,1)}, bf16[392,768]{0,1:T(8,128)(2,1)}, bf16[392,768]{0,1:T(8,128)(2...) while((s32[]{:T(128)}, bf16[256,768]{0,1:T(8,128)(2,1)}, ...), condition=%wide.region_30.31_spmd.clone, body=%wide.region_29.30_spmd.clone.sunk | while | flops 130222080 | bytes 5719823 | solution.py:210
  711.3 19.7 %reduce-scatter.45.cloned.1.call-done = bf16[64,768]{1,0:T(8,128)(2,1)} async-done(((bf16[256,768]{1,0:T(8,128)(2,1)}), bf16[64,768]{1,0:T(8,128)(2,1)}) %reduce-scatter.45.cloned.1.call-update) | async-done | bytes 98320
  736.9 31.6 %while.133 = (s32[]{:T(128)}, bf16[64,768]{0,1:T(8,128)(2,1)S(1)}, bf16[256,768]{0,1:T(8,128)(2,1)S(1)}, bf16[256,768]{0,1:T(8,128)(2,1)S(1)}, bf16[256,768]{0,1...) while((s32[]{:T(128)}, bf16[64,768]{0,1:T(8,128)(2,1)S(1)}, ...), condition=%wide.region_36.37_spmd.clone, body=%wide.region_34.36_spmd.clone.sunk | while | flops 21397380 | bytes 2150875 | solution.py:210
  771.1 3.5 all-to-all-start.9
  777.2 15.4 %all-to-all-done.9 = bf16[8,4,24,768]{3,2,0,1:T(8,128)(2,1)S(1)} async-done(((bf16[8,4,24,768]{3,2,0,1:T(8,128)(2,1)}), bf16[8,4,24,768]{3,2,0,1:T(8,128)(2,1)S(1)}, u32[]{:S(2)}, u32[]{:S(2)}) %all-to-all-start.9) | async-done | bytes 1179680 | tf_op jit(solution)/shard_map/all_to_all | solution.py:481
  795.7 19.8 %all_to_all.60 = bf16[8,4,24,768]{3,2,0,1:T(8,128)(2,1)S(1)} all-to-all(bf16[8,4,24,768]{3,2,0,1:T(8,128)(2,1)S(1)} %copy.184), channel_id=1, replica_groups=mesh['dp'=8,'seq'=4] {'seq'}, dimensions={1} | all-to-all | bytes 2359296 | tf_op jit(solution)/shard_map/all_to_all | solution.py:467
  819.8 3.7 all-to-all-start.8
  826.8 12.5 all-to-all-done.8
  839.3 4.3 all-to-all-start.6
  844.7 2.6 fusion.163
  850.6 8.9 all-to-all-done.6
  859.5 3.5 all-to-all-start.5
  866.4 12.5 all-to-all-done.5
  878.9 3.5 all-to-all-start.4
  882.5 2.3 convert_reduce_fusion.5
  886.5 11.8 all-to-all-done.4
  898.3 4.3 all-to-all-start.3
  904.1 14.3 all-to-all-done.3
  918.4 4.3 all-to-all-start.2
  925.4 2.6 copy.188
  928.0 10.7 all-to-all-done.2
  938.7 5.0 all-to-all-start.10
  944.8 2.4 convert_reduce_fusion.8
  947.2 2.3 convert_reduce_fusion.9
  949.6 47.9 %all-to-all-done.10 = bf16[8,4,24,3072]{3,2,0,1:T(8,128)(2,1)} async-done(((bf16[8,4,24,3072]{3,2,0,1:T(8,128)(2,1)}), bf16[8,4,24,3072]{3,2,0,1:T(8,128)(2,1)}, u32[]{:S(2)}, u32[]{:S(2)}) %all-to-all-start.10) | async-done | bytes 4718624 | tf_op jit(solution)/shard_map/all_to_all | solution.py:488
  997.5 4.8 convert_reduce_fusion.1
  1005.6 56.4 %all_to_all.61 = bf16[8,4,96,768]{3,2,0,1:T(8,128)(2,1)S(1)} all-to-all(bf16[8,4,96,768]{3,2,0,1:T(8,128)(2,1)S(1)} %copy.190), channel_id=1, replica_groups=mesh['dp'=8,'seq'=4] {'seq'}, dimensions={1} | all-to-all | bytes 9437184 | tf_op jit(solution)/shard_map/all_to_all | solution.py:495
  1069.1 5.6 all-to-all-start.1
  1074.8 5.2 fusion.61
  1080.0 12.5 all-to-all-done.1
  1095.2 39.2 %all-reduce.20 = (f32[3072]{0:T(1024)S(1)}, f32[768]{0:T(1024)S(1)}, f32[768]{0:T(1024)S(1)}, f32[768]{0:T(1024)S(1)}, f32[768]{0:T(1024)S(1)}, /*index=5*/f32[7...) all-reduce(f32[3072]{0:T(1024)S(1)} %copy-done.70, ...), channel_id=18, replica_groups=mesh['dp'=8,'seq'=4] {'dp','seq'}, use_global_device_ids=true, to_apply=%region_64.65.clone | all-reduce | flops 9984 | bytes 79872
  1140.2 5.8 reduce-scatter.29.cloned.1.call-done
  1146.0 65.2 %reduce-scatter.27.cloned.1.call-done = f32[24,768]{1,0:T(8,128)} async-done(((f32[192,768]{1,0:T(8,128)}), f32[24,768]{1,0:T(8,128)}) %reduce-scatter.27.cloned.1.call-update) | async-done | bytes 73744 | tf_op jit(solution)/shard_map/reduce_scatter | solution.py:507
  1211.2 65.0 %reduce-scatter.25.cloned.1.call-done = f32[24,768]{1,0:T(8,128)} async-done(((f32[192,768]{1,0:T(8,128)}), f32[24,768]{1,0:T(8,128)}) %reduce-scatter.25.cloned.1.call-update) | async-done | bytes 73744 | tf_op jit(solution)/shard_map/reduce_scatter | solution.py:506
  1276.2 65.4 %reduce-scatter.23.cloned.1.call-done = f32[24,768]{1,0:T(8,128)} async-done(((f32[192,768]{1,0:T(8,128)}), f32[24,768]{1,0:T(8,128)}) %reduce-scatter.23.cloned.1.call-update) | async-done | bytes 73744 | tf_op jit(solution)/shard_map/reduce_scatter | solution.py:505
  1341.6 72.2 %reduce-scatter.39.cloned.1.call-done = f32[24,3072]{1,0:T(8,128)} async-done(((f32[192,3072]{1,0:T(8,128)}), f32[24,3072]{1,0:T(8,128)}) %reduce-scatter.39.cloned.1.call-update) | async-done | bytes 294928 | tf_op jit(solution)/shard_map/reduce_scatter | solution.py:513
  1413.8 72.1 %reduce-scatter.41.cloned.1.call-done = f32[96,768]{1,0:T(8,128)} async-done(((f32[768,768]{1,0:T(8,128)}), f32[96,768]{1,0:T(8,128)}) %reduce-scatter.41.cloned.1.call-update) | async-done | bytes 294928 | tf_op jit(solution)/shard_map/reduce_scatter | solution.py:514
  (770 shorter events, 213.4 us)
Async XLA Ops:
  7.2 60.3 %copy-start.1 = (bf16[4,49,768]{2,0,1:T(4,128)(2,1)S(1)}, bf16[4,49,768]{2,0,1:T(4,128)(2,1)}, u32[]{:S(2)}) copy-start(bf16[4,49,768]{2,0,1:T(4,128)(2,1)} %param.40) | copy-start | bytes 903172
  7.2 84.5 %all-gather.13.cloned.1.call-start = ((), (), s32[]{:S(2)}) async-start(), calls=%async_computation.26 | async-start | bytes 1216512 | tf_op jit(solution)/shard_map/all_gather | solution.py:261
  7.9 116.9 %all-gather.17.cloned.1.call-start = ((), (), s32[]{:S(2)}) async-start(), calls=%async_computation.28 | async-start | bytes 1216512 | tf_op jit(solution)/shard_map/all_gather | solution.py:260
  8.7 172.1 %all-gather.15.cloned.1.call-start = ((), (), s32[]{:S(2)}) async-start(), calls=%async_computation.27 | async-start | bytes 1216512 | tf_op jit(solution)/shard_map/all_gather | solution.py:259
  9.4 227.2 %all-gather.19.cloned.1.call-start = ((), (), s32[]{:S(2)}) async-start(), calls=%async_computation.29 | async-start | bytes 1216512 | tf_op jit(solution)/shard_map/all_gather | solution.py:262
  10.0 282.4 %all-gather.23.cloned.1.call-start = ((), (), s32[]{:S(2)}) async-start(), calls=%async_computation.31 | async-start | bytes 1216512 | tf_op jit(solution)/shard_map/all_gather | solution.py:263
  10.6 337.5 %all-gather.25.cloned.1.call-start = ((), (), s32[]{:S(2)}) async-start(), calls=%async_computation.32 | async-start | bytes 1216512 | tf_op jit(solution)/shard_map/all_gather | solution.py:264
  11.2 392.8 %all-gather.21.cloned.1.call-start = ((), (), s32[]{:S(2)}) async-start(), calls=%async_computation.30 | async-start | bytes 1216512 | tf_op jit(solution)/shard_map/all_gather | solution.py:265
  69.1 22.4 %all-to-all-start = ((bf16[8,49,768]{2,1,0:T(8,128)(2,1)}), bf16[8,49,768]{2,1,0:T(8,128)(2,1)S(1)}, u32[]{:S(2)}, u32[]{:S(2)}) async-start(bf16[8,49,768]{2,1,0:T(8,128)(2,1)} %copy.156), calls=%async_computation | async-start | bytes 1376256 | tf_op jit(solution)/shard_map/all_to_all | solution.py:338
  74.2 385.7 %all-gather.27.cloned.1.call-start = ((), (), s32[]{:S(2)}) async-start(), calls=%async_computation.33 | async-start | bytes 1216512 | tf_op jit(solution)/shard_map/all_gather | solution.py:266
  74.9 407.2 %reduce-scatter.43.cloned.1.call-start = ((), (), s32[]{:S(2)}) async-start(), calls=%async_computation.46 | async-start | bytes 491520
  75.0 105.7 %copy-start.43 = (f32[768]{0:T(1024)}, f32[768]{0:T(1024)S(1)}, u32[]{:S(2)}) copy-start(f32[768]{0:T(1024)S(1)} %convert_element_type.281) | copy-start | bytes 9220
  75.1 217.3 %copy-start.45 = (f32[768]{0:T(1024)}, f32[768]{0:T(1024)S(1)}, u32[]{:S(2)}) copy-start(f32[768]{0:T(1024)S(1)} %convert_element_type.293) | copy-start | bytes 9220
  75.1 217.3 %copy-start.53 = (f32[768]{0:T(1024)}, f32[768]{0:T(1024)S(1)}, u32[]{:S(2)}) copy-start(f32[768]{0:T(1024)S(1)} %convert_element_type.294) | copy-start | bytes 9220
  75.5 105.3 %copy-start.55 = (f32[64]{0:T(128)}, f32[64]{0:T(128)S(1)}, u32[]{:S(2)}) copy-start(f32[64]{0:T(128)S(1)} %broadcast_multiply_fusion.3) | copy-start | bytes 772
  75.7 17.9 %copy-start.77 = (f32[64]{0:T(128)}, f32[64]{0:T(128)S(1)}, u32[]{:S(2)}) copy-start(f32[64]{0:T(128)S(1)} %fusion.122) | copy-start | bytes 772
  75.7 105.1 %copy-start.68 = (f32[64]{0:T(128)}, f32[64]{0:T(128)S(1)}, u32[]{:S(2)}) copy-start(f32[64]{0:T(128)S(1)} %fusion.143) | copy-start | bytes 772
  91.7 312.3 %copy-start.14 = (bf16[392,768]{1,0:T(8,128)(2,1)}, bf16[392,768]{1,0:T(8,128)(2,1)S(1)}, u32[]{:S(2)}) copy-start(bf16[392,768]{1,0:T(8,128)(2,1)S(1)} %reshape.556) | copy-start | bytes 1806340
  191.4 45.2 %copy-start.12 = (bf16[256,768]{0,1:T(8,128)(2,1)}, bf16[256,768]{0,1:T(8,128)(2,1)S(1)}, u32[]{:S(2)}) copy-start(bf16[256,768]{0,1:T(8,128)(2,1)S(1)} %get-tuple-element.2766) | copy-start | bytes 1179652
  191.4 100.9 %copy-start.31 = (bf16[64,768]{1,0:T(8,128)(2,1)}, bf16[64,768]{1,0:T(8,128)(2,1)S(1)}, u32[]{:S(2)}) copy-start(bf16[64,768]{1,0:T(8,128)(2,1)S(1)} %get-tuple-element.2800) | copy-start | bytes 294916
  191.4 100.9 %copy-start.49 = (s32[64]{0:T(128)}, s32[64]{0:T(128)S(1)}, u32[]{:S(2)}) copy-start(s32[64]{0:T(128)S(1)} %get-tuple-element.2810) | copy-start | bytes 772
  191.4 102.6 %copy-start.13 = (bf16[256,768]{0,1:T(8,128)(2,1)}, bf16[256,768]{0,1:T(8,128)(2,1)S(1)}, u32[]{:S(2)}) copy-start(bf16[256,768]{0,1:T(8,128)(2,1)S(1)} %get-tuple-element.2767) | copy-start | bytes 1179652
  191.4 102.6 %copy-start.16 = (bf16[64,768]{0,1:T(8,128)(2,1)}, bf16[64,768]{0,1:T(8,128)(2,1)S(1)}, u32[]{:S(2)}) copy-start(bf16[64,768]{0,1:T(8,128)(2,1)S(1)} %get-tuple-element.1483) | copy-start | bytes 294916
  238.4 54.0 %copy-start.64 = (f32[64]{0:T(128)}, f32[64]{0:T(128)S(1)}, u32[]{:S(2)}) copy-start(f32[64]{0:T(128)S(1)} %broadcast_multiply_fusion.2) | copy-start | bytes 772
  238.6 62.2 %copy-start.79 = (f32[64]{0:T(128)}, f32[64]{0:T(128)S(1)}, u32[]{:S(2)}) copy-start(f32[64]{0:T(128)S(1)} %multiply_reduce_fusion.6) | copy-start | bytes 772
  238.6 53.8 %copy-start.71 = (f32[64]{0:T(128)}, f32[64]{0:T(128)S(1)}, u32[]{:S(2)}) copy-start(f32[64]{0:T(128)S(1)} %fusion.144) | copy-start | bytes 772
  413.2 70.8 %copy-start.24 = (f32[6,2,256]{2,1,0:T(2,128)}, f32[6,2,256]{2,1,0:T(2,128)S(1)}, u32[]{:S(2)}) copy-start(f32[6,2,256]{2,1,0:T(2,128)S(1)} %get-tuple-element.2796) | copy-start | bytes 36868
  413.2 70.8 %copy-start.25 = (f32[6,2,256]{2,1,0:T(2,128)}, f32[6,2,256]{2,1,0:T(2,128)S(1)}, u32[]{:S(2)}) copy-start(f32[6,2,256]{2,1,0:T(2,128)S(1)} %get-tuple-element.2798) | copy-start | bytes 36868
  413.2 70.8 %copy-start.81 = (pred[8]{0:T(512)(128)(4,1)}, pred[8]{0:T(512)(128)(4,1)S(1)}, u32[]{:S(2)}) copy-start(pred[8]{0:T(512)(128)(4,1)S(1)} %get-tuple-element.2828) | copy-start | bytes 28
  414.1 134.5 %all-gather.29.cloned.1.call-start = ((), (), s32[]{:S(2)}) async-start(), calls=%async_computation.34 | async-start | bytes 4866048 | tf_op jit(solution)/shard_map/all_gather | solution.py:267
  414.7 199.3 %all-gather.31.cloned.1.call-start = ((), (), s32[]{:S(2)}) async-start(), calls=%async_computation.35 | async-start | bytes 4866048 | tf_op jit(solution)/shard_map/all_gather | solution.py:268
  415.5 315.5 %reduce-scatter.45.cloned.1.call-start = ((), (), s32[]{:S(2)}) async-start(), calls=%async_computation.47 | async-start | bytes 491520
  415.7 138.7 %copy-start.47 = (f32[768]{0:T(1024)}, f32[768]{0:T(1024)S(1)}, u32[]{:S(2)}) copy-start(f32[768]{0:T(1024)S(1)} %convert_element_type.300) | copy-start | bytes 9220
  484.0 138.2 %copy-start.66 = (f32[64]{0:T(128)}, f32[64]{0:T(128)S(1)}, u32[]{:S(2)}) copy-start(f32[64]{0:T(128)S(1)} %broadcast_multiply_fusion.1) | copy-start | bytes 772
  484.2 138.0 %copy-start.73 = (f32[64]{0:T(128)}, f32[64]{0:T(128)S(1)}, u32[]{:S(2)}) copy-start(f32[64]{0:T(128)S(1)} %fusion.145) | copy-start | bytes 772
  484.2 129.8 %copy-start.28 = (bf16[1,64,768]{2,1,0:T(8,128)(2,1)S(1)}, bf16[1,64,768]{2,1,0:T(8,128)(2,1)}, u32[]{:S(2)}) copy-start(bf16[1,64,768]{2,1,0:T(8,128)(2,1)} %param.43) | copy-start | bytes 294916
  709.2 21.9 %copy-start.5 = (bf16[768,768]{1,0:T(8,128)(2,1)S(1)}, bf16[768,768]{1,0:T(8,128)(2,1)}, u32[]{:S(2)}) copy-start(bf16[768,768]{1,0:T(8,128)(2,1)} %all-gather.23.cloned.1.call-done) | copy-start | bytes 3538948
  711.2 23.5 %copy-start.19 = (f32[64,768]{1,0:T(8,128)S(1)}, f32[64,768]{1,0:T(8,128)}, u32[]{:S(2)}) copy-start(f32[64,768]{1,0:T(8,128)} %copy-done.18) | copy-start | bytes 589828
  711.2 133.5 %reduce-scatter.47.cloned.1.call-start = ((), (), s32[]{:S(2)}) async-start(), calls=%async_computation.48 | async-start | bytes 491520
  711.3 25.0 %copy-start.4 = (bf16[768,768]{1,0:T(8,128)(2,1)S(1)}, bf16[768,768]{1,0:T(8,128)(2,1)}, u32[]{:S(2)}) copy-start(bf16[768,768]{1,0:T(8,128)(2,1)} %all-gather.19.cloned.1.call-done) | copy-start | bytes 3538948
  771.1 21.5 %all-to-all-start.9 = ((bf16[8,4,24,768]{3,2,0,1:T(8,128)(2,1)}), bf16[8,4,24,768]{3,2,0,1:T(8,128)(2,1)S(1)}, u32[]{:S(2)}, u32[]{:S(2)}) async-start(bf16[8,4,24,768]{3,2,0,1:T(8,128)(2,1)} %copy.187), calls=%async_computation.16 | async-start | bytes 2359296 | tf_op jit(solution)/shard_map/all_to_all | solution.py:481
  774.7 72.7 %reduce-scatter.49.cloned.1.call-start = ((), (), s32[]{:S(2)}) async-start(), calls=%async_computation.49 | async-start | bytes 491520
  775.7 364.5 %reduce-scatter.37.cloned.1.call-start = ((), (), s32[]{:S(2)}) async-start(), calls=%async_computation.43 | async-start | bytes 663552 | tf_op jit(solution)/shard_map/reduce_scatter | solution.py:512
  777.2 16.5 %copy-start.8 = (bf16[392,768]{0,1:T(8,128)(2,1)S(1)}, bf16[392,768]{0,1:T(8,128)(2,1)}, u32[]{:S(2)}) copy-start(bf16[392,768]{0,1:T(8,128)(2,1)} %get-tuple-element.1496) | copy-start | bytes 1806340
  793.6 346.5 %reduce-scatter.33.cloned.1.call-start = ((), (), s32[]{:S(2)}) async-start(), calls=%async_computation.41 | async-start | bytes 663552 | tf_op jit(solution)/shard_map/reduce_scatter | solution.py:510
  819.8 19.5 %all-to-all-start.8 = ((bf16[8,4,24,768]{3,2,0,1:T(8,128)(2,1)}), bf16[8,4,24,768]{3,2,0,1:T(8,128)(2,1)S(1)}, u32[]{:S(2)}, u32[]{:S(2)}) async-start(bf16[8,4,24,768]{3,2,0,1:T(8,128)(2,1)} %copy.186), calls=%async_computation.14 | async-start | bytes 2359296 | tf_op jit(solution)/shard_map/all_to_all | solution.py:474
  839.3 20.2 %all-to-all-start.6 = ((bf16[8,4,24,768]{3,2,0,1:T(8,128)(2,1)}), bf16[8,4,24,768]{3,2,0,1:T(8,128)(2,1)}, u32[]{:S(2)}, u32[]{:S(2)}) async-start(bf16[8,4,24,768]{3,2,0,1:T(8,128)(2,1)} %copy.181), calls=%async_computation.10 | async-start | bytes 2359296 | tf_op jit(solution)/shard_map/all_to_all | solution.py:460
  843.6 296.6 %reduce-scatter.35.cloned.1.call-start = ((), (), s32[]{:S(2)}) async-start(), calls=%async_computation.42 | async-start | bytes 663552 | tf_op jit(solution)/shard_map/reduce_scatter | solution.py:511
  859.5 19.4 %all-to-all-start.5 = ((bf16[8,4,24,768]{3,2,0,1:T(8,128)(2,1)}), bf16[8,4,24,768]{3,2,0,1:T(8,128)(2,1)S(1)}, u32[]{:S(2)}, u32[]{:S(2)}) async-start(bf16[8,4,24,768]{3,2,0,1:T(8,128)(2,1)} %copy.180), calls=%async_computation.8 | async-start | bytes 2359296 | tf_op jit(solution)/shard_map/all_to_all | solution.py:453
  878.9 19.4 %all-to-all-start.4 = ((bf16[8,4,24,768]{3,2,0,1:T(8,128)(2,1)}), bf16[8,4,24,768]{3,2,0,1:T(8,128)(2,1)S(1)}, u32[]{:S(2)}, u32[]{:S(2)}) async-start(bf16[8,4,24,768]{3,2,0,1:T(8,128)(2,1)} %copy.179), calls=%async_computation.6 | async-start | bytes 2359296 | tf_op jit(solution)/shard_map/all_to_all | solution.py:446
  882.4 257.8 %reduce-scatter.31.cloned.1.call-start = ((), (), s32[]{:S(2)}) async-start(), calls=%async_computation.40 | async-start | bytes 663552 | tf_op jit(solution)/shard_map/reduce_scatter | solution.py:509
  898.3 20.2 %all-to-all-start.3 = ((bf16[8,4,24,768]{3,2,0,1:T(8,128)(2,1)}), bf16[8,4,24,768]{3,2,0,1:T(8,128)(2,1)}, u32[]{:S(2)}, u32[]{:S(2)}) async-start(bf16[8,4,24,768]{3,2,0,1:T(8,128)(2,1)} %copy.177), calls=%async_computation.4 | async-start | bytes 2359296 | tf_op jit(solution)/shard_map/all_to_all | solution.py:439
  918.4 20.2 %all-to-all-start.2 = ((bf16[8,4,24,768]{3,2,0,1:T(8,128)(2,1)}), bf16[8,4,24,768]{3,2,0,1:T(8,128)(2,1)}, u32[]{:S(2)}, u32[]{:S(2)}) async-start(bf16[8,4,24,768]{3,2,0,1:T(8,128)(2,1)} %copy.175), calls=%async_computation.2 | async-start | bytes 2359296 | tf_op jit(solution)/shard_map/all_to_all | solution.py:432
  922.8 223.2 %reduce-scatter.29.cloned.1.call-start = ((), (), s32[]{:S(2)}) async-start(), calls=%async_computation.39 | async-start | bytes 663552 | tf_op jit(solution)/shard_map/reduce_scatter | solution.py:508
  938.7 58.8 %all-to-all-start.10 = ((bf16[8,4,24,3072]{3,2,0,1:T(8,128)(2,1)}), bf16[8,4,24,3072]{3,2,0,1:T(8,128)(2,1)}, u32[]{:S(2)}, u32[]{:S(2)}) async-start(bf16[8,4,24,3072]{3,2,0,1:T(8,128)(2,1)} %copy.188), calls=%async_computation.18 | async-start | bytes 9437184 | tf_op jit(solution)/shard_map/all_to_all | solution.py:488
  943.6 267.6 %reduce-scatter.27.cloned.1.call-start = ((), (), s32[]{:S(2)}) async-start(), calls=%async_computation.38 | async-start | bytes 663552 | tf_op jit(solution)/shard_map/reduce_scatter | solution.py:507
  944.7 331.4 %reduce-scatter.25.cloned.1.call-start = ((), (), s32[]{:S(2)}) async-start(), calls=%async_computation.37 | async-start | bytes 663552 | tf_op jit(solution)/shard_map/reduce_scatter | solution.py:506
  947.2 394.4 %reduce-scatter.23.cloned.1.call-start = ((), (), s32[]{:S(2)}) async-start(), calls=%async_computation.36 | async-start | bytes 663552 | tf_op jit(solution)/shard_map/reduce_scatter | solution.py:505
  949.6 464.2 %reduce-scatter.39.cloned.1.call-start = ((), (), s32[]{:S(2)}) async-start(), calls=%async_computation.44 | async-start | bytes 2654208 | tf_op jit(solution)/shard_map/reduce_scatter | solution.py:513
  1002.3 483.5 %reduce-scatter.41.cloned.1.call-start = ((), (), s32[]{:S(2)}) async-start(), calls=%async_computation.45 | async-start | bytes 2654208 | tf_op jit(solution)/shard_map/reduce_scatter | solution.py:514
  1069.1 23.3 %all-to-all-start.1 = ((bf16[8,49,768]{2,1,0:T(8,128)(2,1)}), bf16[8,49,768]{2,1,0:T(8,128)(2,1)S(1)}, u32[]{:S(2)}, u32[]{:S(2)}) async-start(bf16[8,49,768]{2,1,0:T(8,128)(2,1)} %reshape.557), calls=%async_computation.1 | async-start | bytes 1376256 | tf_op jit(solution)/shard_map/all_to_all | solution.py:392
  1074.7 17.7 %copy-start.33 = (f32[4,49]{0,1:T(8,128)S(1)}, f32[4,49]{0,1:T(8,128)}, u32[]{:S(2)}) copy-start(f32[4,49]{0,1:T(8,128)} %copy-done.32) | copy-start | bytes 2356
  1074.7 17.7 %copy-start.52 = (f32[768]{0:T(1024)S(1)}, f32[768]{0:T(1024)}, u32[]{:S(2)}) copy-start(f32[768]{0:T(1024)} %copy-done.51) | copy-start | bytes 9220
  1074.7 17.7 %copy-start.84 = (s32[4]{0:T(128)S(1)}, s32[4]{0:T(128)}, u32[]{:S(2)}) copy-start(s32[4]{0:T(128)} %copy-done.83) | copy-start | bytes 52
  (56 other events, 220.7 us)
Sparse Core Ops, SparseCore 0:
  10.9 56.7 all-gather.12
  70.7 54.1 all-gather.16
  127.8 52.9 all-gather.14
  183.5 53.0 all-gather.18
  239.3 52.9 all-gather.22
  295.1 52.9 all-gather.24
  351.0 52.9 all-gather.20
  406.9 52.9 all-gather.26
  462.4 19.7 reduce-scatter.42
  484.9 63.6 all-gather.28
  551.5 62.4 all-gather.30
  711.3 19.6 reduce-scatter.44
  769.6 23.0 reduce-scatter.46
  795.1 21.9 reduce-scatter.48
  820.7 62.0 reduce-scatter.36
  887.0 61.1 reduce-scatter.32
  951.9 61.0 reduce-scatter.34
  1017.0 61.2 reduce-scatter.30
  1082.2 63.7 reduce-scatter.28
  1150.1 61.0 reduce-scatter.26
  1215.1 61.0 reduce-scatter.24
  1280.4 61.1 reduce-scatter.22
  1345.6 68.0 reduce-scatter.38
  1417.7 68.0 reduce-scatter.40
where the time goes:
time: 1510 us; the launch traced here: 1490 us
  waiting for transfers between devices  981 us (65%)
  blocking collectives  208 us (14%)
  local copies, waits for them, and re-layouts  122 us (8%)
  matrix products  86.2 us (6%)
  starting transfers between devices  44.3 us (3%)
  other arithmetic  33.6 us (2%)
  between operations  16.3 us (1%)
    unnamed x2, blocking collectives  81.8 us
    reduce_scatter x1, waiting for transfers between devices, per_device(): lax.psum_scatter(folded[8], 'dp', scatter_dimension=0, tiled=True)  72.2 us
    reduce_scatter x1, waiting for transfers between devices, per_device(): lax.psum_scatter(folded[9], 'dp', scatter_dimension=0, tiled=True)  72.1 us
    reduce_scatter x1, waiting for transfers between devices, per_device(): lax.psum_scatter(folded[0], 'dp', scatter_dimension=0, tiled=True)  65.4 us
    reduce_scatter x1, waiting for transfers between devices, per_device(): lax.psum_scatter(folded[2], 'dp', scatter_dimension=0, tiled=True)  65.2 us
    reduce_scatter x1, waiting for transfers between devices, per_device(): lax.psum_scatter(folded[1], 'dp', scatter_dimension=0, tiled=True)  65 us
    all_gather x1, waiting for transfers between devices, per_device(): lax.all_gather(w_up, ('dp', 'seq'), axis=0, tiled=True)  64.4 us
    all_gather x1, waiting for transfers between devices, per_device(): lax.all_gather(w_down, ('dp', 'seq'), axis=0, tiled=True)  59.6 us
  transfers between devices with their start and end apart: 34, of which 27 were waited for; matrix products, arithmetic and copies ran while one was open for 8% of the time, Pallas kernels for 0%

commit v1 on v0

--- a/solution.py
+++ b/solution.py
@@ -1,12 +1,17 @@
 from functools import partial
 import math
+from types import SimpleNamespace
 
 import jax
 import jax.numpy as jnp
 from jax import lax
+from jax.experimental import pallas as pl
+from jax.experimental.pallas import tpu as pltpu
 from jax.sharding import PartitionSpec as P
 
 HEAD = 64
+LANES = 128
+MESH = pl.DeviceIdType.MESH
 
 
 EPSILON = 1e-05
@@ -528,6 +533,1115 @@
     return (text_out, text_grad, image_grad) + tuple(summed_mats) + tuple(summed_vecs)
 
 
+def dot_plain(former, latter):
+    return jnp.dot(former, latter, preferred_element_type=jnp.float32)
+
+
+def dot_right(former, latter):
+    return lax.dot_general(
+        former, latter, (((1,), (1,)), ((), ())), preferred_element_type=jnp.float32
+    )
+
+
+def dot_left(former, latter):
+    return lax.dot_general(
+        former, latter, (((0,), (0,)), ((), ())), preferred_element_type=jnp.float32
+    )
+
+
+def low(values):
+    return values.astype(jnp.bfloat16)
+
+
+def wide(values):
+    return values.astype(jnp.float32)
+
+
+def block(index, size):
+    if isinstance(index, int):
+        return pl.ds(index * size, size)
+    return pl.ds(pl.multiple_of(index * size, size), size)
+
+
+def lanes(start, size):
+    return pl.ds(start, size)
+
+
+def norm_parts(values):
+    average = jnp.mean(values, axis=-1, keepdims=True)
+    centered = values - average
+    spread = jnp.mean(centered * centered, axis=-1, keepdims=True)
+    inverse = lax.rsqrt(spread + EPSILON)
+    return centered * inverse, inverse
+
+
+def norm_back(unit, inverse, gain_row, grad):
+    scaled = grad * gain_row
+    first = jnp.mean(scaled, axis=-1, keepdims=True)
+    second = jnp.mean(scaled * unit, axis=-1, keepdims=True)
+    return (scaled - first - unit * second) * inverse
+
+
+def column_sum(values):
+    return jnp.sum(values, axis=0, keepdims=True)
+
+
+class Copies:
+    def __init__(self, send_sems, recv_sems):
+        self.send_sems, self.recv_sems = send_sems, recv_sems
+        self.count = 0
+        self.started = []
+
+    def make(self, source, target, device):
+        index = self.count
+        self.count += 1
+        return pltpu.make_async_remote_copy(
+            src_ref=source,
+            dst_ref=target,
+            send_sem=self.send_sems.at[index],
+            recv_sem=self.recv_sems.at[index],
+            device_id=device,
+            device_id_type=MESH,
+        )
+
+    def begin(self, source, target, device):
+        copy = self.make(source, target, device)
+        copy.start()
+        self.started.append(copy)
+        return copy
+
+
+COPY_SLOTS = 256
+
+
+def scratch_of(width, tokens, seq_count, data_count, hidden, main, shard):
+    length = tokens * seq_count
+    band = shard * seq_count
+    inbox = data_count * main
+    rests = seq_count * data_count
+    keys = inbox * seq_count + rests
+    bf16, f32 = jnp.bfloat16, jnp.float32
+    return dict(
+        vec_own=((16, LANES), f32),
+        vec_all=((data_count, seq_count, 16, LANES), bf16),
+        vec=((16, width), f32),
+        up_bias=((1, hidden), f32),
+        key_bias=((1, keys), f32),
+        slab_out=((seq_count, shard, 1152 + hidden), bf16),
+        slab_in=((seq_count, shard, 1152 + hidden), bf16),
+        cols=((width, 1152 + hidden), bf16),
+        halves=((width, 768), bf16),
+        cot_all=((length, width), bf16),
+        h1=((length, width), bf16),
+        h2=((length, width), bf16),
+        h3=((length, width), bf16),
+        e1=((length, width), bf16),
+        e2=((length, width), bf16),
+        out_all=((data_count, shard, 2 * width), bf16),
+        out_in=((seq_count, data_count // seq_count, shard, 2 * width), bf16),
+        out_rows=((256, 2 * width), bf16),
+        down_all=((hidden, width), bf16),
+        outbox=((inbox, width), bf16),
+        rest_rows=((data_count, width), f32),
+        rest_wide=((rests * 16, LANES), f32),
+        rest_out=((data_count, 16, LANES), bf16),
+        rest_in=((seq_count, data_count, 16, LANES), bf16),
+        tiles=((keys, width), bf16),
+        kv2=((keys, 512), bf16),
+        dkv2=((keys, 512), bf16),
+        qm1=((3 * length, LANES), bf16),
+        qm2=((3 * length, LANES), bf16),
+        dom=((3 * length, LANES), bf16),
+        qkv1=((length, 768), bf16),
+        p1=((3 * length, length), f32),
+        o1=((length, 256), bf16),
+        o2=((length, 256), bf16),
+        o_acc=((length, 256), f32),
+        ds=((3 * length, keys), bf16),
+        pr=((3 * length, keys), bf16),
+        sums_out=((6, 3, tokens, width), bf16),
+        sums_in=((6, 3, tokens, width), bf16),
+        x2=((tokens, width), f32),
+        x3=((tokens, width), f32),
+        dx=((tokens, width), f32),
+        act=((length, hidden), bf16),
+        slope=((length, hidden), f32),
+        du=((length, hidden), bf16),
+        dqkv=((length, 768), bf16),
+        dq2=((length, 256), bf16),
+        dn=((keys, width), bf16),
+        dn_pair=((2, inbox, width), bf16),
+        dn_far=((inbox, width), bf16),
+        dn_home=((inbox, width), bf16),
+        dr_out=((seq_count, data_count, 16, LANES), bf16),
+        dr_pair=((2, data_count, 16, LANES), bf16),
+        dr_far=((data_count, 16, LANES), bf16),
+        dr_home=((data_count, 16, LANES), bf16),
+        g_cols=((width, 1152 + hidden), bf16),
+        g_half=((width, 384), bf16),
+        g_half2=((width, 384), bf16),
+        half_in=((width, 384), bf16),
+        g_down=((hidden, width), bf16),
+        g_out=((data_count, shard, 2 * width), bf16),
+        g_out_send=((2, seq_count, data_count // seq_count, shard, width), bf16),
+        y_up=((4, band, hidden), bf16),
+        z_up=((3, band, hidden), bf16),
+        y_down=((4, band, width), bf16),
+        z_down=((3, band, width), bf16),
+        y_cross=((4, band, 384), bf16),
+        z_cross=((3, band, 384), bf16),
+        y_self=((4, band, 768), bf16),
+        z_self=((3, band, 768), bf16),
+        y_xout=((4, shard, width), bf16),
+        z_xout=((3, shard, width), bf16),
+        y_sout=((4, shard, width), bf16),
+        z_sout=((3, shard, width), bf16),
+        cols_out=((seq_count, shard, 1152 + hidden), bf16),
+        cols_in=((seq_count, shard, 1152 + hidden), bf16),
+        vv=((16, width), f32),
+        vv_out=((data_count, 16, LANES), f32),
+        vv_in=((data_count, 16, LANES), f32),
+        vq=((seq_count, 16, LANES), f32),
+    )
+
+
+def lane_pick(parts, lane):
+    result = None
+    for source, first, place, size in parts:
+        start = first // LANES * LANES
+        stop = start + LANES * (1 if first + size <= start + LANES else 2)
+        window = source[:, start:stop]
+        turn = (place - first + start) % (stop - start)
+        if turn:
+            window = pltpu.roll(window, turn, 1)
+        window = window[:, 0:LANES]
+        if result is None:
+            result = window
+        else:
+            result = jnp.where((lane >= place) & (lane < place + size), window, result)
+    return result
+
+
+def spans(start, stop, size):
+    while start < stop:
+        end = min(stop, (start // size + 1) * size)
+        yield start, end - start
+        start = end
+
+
+def fused_kernel(names, n_in, *refs):
+    (
+        slide, owner, text, img, cot, w_query, w_key, w_value, w_out, c_query, c_key, c_value,
+        c_out, w_up, w_down, b_up, b_down, *gains,
+    ) = refs[:n_in]
+    r_text, r_tgrad, r_igrad, r_cols, r_outs, r_down, r_vec = refs[n_in : n_in + 7]
+    m = SimpleNamespace(**dict(zip(names, refs[n_in + 7 :])))
+    links = Copies(m.send, m.recv)
+    begin = links.begin
+
+    _, tokens, width = text.shape
+    seq_count = m.slab_out.shape[0]
+    length = tokens * seq_count
+    shard = w_out.shape[0]
+    data_count = m.vec_all.shape[0]
+    hidden = m.down_all.shape[0]
+    band = shard * seq_count
+    tile_count, real_rows, _ = img.shape
+    slides = owner.shape[0]
+    main = real_rows // 16 * 16
+    inbox = data_count * main
+    keys_main = inbox * seq_count
+    rests = seq_count * data_count
+    keys = keys_main + rests
+    columns = width // LANES
+    factor = 1.0 / math.sqrt(HEAD)
+    z_count = data_count // 2
+
+    d = lax.axis_index("dp")
+    s = lax.axis_index("seq")
+    z, y = d // 2, d % 2
+    core = s % 2
+    sibling = s + 1 - 2 * core
+    across = (s + 2) % 4
+    corner = 3 - s
+    seq_peers = [sibling, across, corner]
+    z_peers = [(z + k) % z_count for k in range(1, z_count)]
+    z_from = [(z + z_count - k) % z_count for k in range(1, z_count)]
+    near = (z * 2 + 1 - y, s)
+
+    barrier = pltpu.get_barrier_semaphore()
+    for peer in seq_peers:
+        pl.semaphore_signal(barrier, inc=1, device_id=(d, peer), device_id_type=MESH)
+    for k in range(1, data_count):
+        pl.semaphore_signal(
+            barrier, inc=1, device_id=((d + k) % data_count, s), device_id_type=MESH
+        )
+
+    lane = lax.broadcasted_iota(jnp.int32, (1, LANES), 1)
+    head_masks = [
+        jnp.where(lane < HEAD, 1.0, 0.0),
+        jnp.where(lane >= HEAD, 1.0, 0.0),
+        jnp.where(lane // HEAD == core, 1.0, 0.0),
+    ]
+
+    def arrive(copies):
+        for copy in copies:
+            copy.wait_recv()
+
+    def seq_gather(views):
+        own = [view(s) for view in views]
+        pair = [begin(part, part, (d, sibling)) for part in own]
+        far = [begin(part, part, (d, across)) for part in own]
+        return views, pair, far
+
+    def seq_pass(state):
+        arrive(state[2])
+        for part in [view(across) for view in state[0]]:
+            state[1].append(begin(part, part, (d, sibling)))
+
+    def seq_end(state):
+        arrive(state[1])
+
+    def rows_of(ref):
+        return [lambda index: ref.at[block(index, tokens)]]
+
+    def gather_far(view):
+        own = view(d)
+        return view, [begin(own, own, (peer * 2 + y, s)) for peer in z_peers], []
+
+    def gather_near(state):
+        own = state[0](d)
+        state[2].append(begin(own, own, near))
+
+    def gather_step(state, k):
+        view, far, close = state
+        far[k].wait_recv()
+        part = view(z_from[k] * 2 + y)
+        close.append(begin(part, part, near))
+
+    def gather_forward(state):
+        for k in range(z_count - 1):
+            gather_step(state, k)
+
+    def gather_end(state):
+        arrive(state[2])
+
+    def seq_sum_begin(slot, produce):
+        both = low(produce(sibling, corner))
+        m.sums_out[slot, 0] = both[0:tokens]
+        m.sums_out[slot, 1] = both[tokens : 2 * tokens]
+        pair = pl.ds(0, 2)
+        copy = begin(m.sums_out.at[slot, pair], m.sums_in.at[slot, pair], (d, sibling))
+        both = produce(across, s)
+        return slot, copy, both[0:tokens], both[tokens : 2 * tokens]
+
+    def seq_sum_pass(state):
+        slot, copy, far, own = state
+        copy.wait_recv()
+        m.sums_out[slot, 2] = low(far + wide(m.sums_in[slot, 1]))
+        return slot, begin(m.sums_out.at[slot, 2], m.sums_in.at[slot, 2], (d, across)), own
+
+    def seq_sum_end(state):
+        slot, copy, own = state
+        own = own + wide(m.sums_in[slot, 0])
+        copy.wait_recv()
+        return own + wide(m.sums_in[slot, 2])
+
+    def pick(ref, first, second, place=slice(None)):
+        return jnp.concatenate(
+            [ref[block(first, tokens), place], ref[block(second, tokens), place]], axis=0
+        )
+
+    def sum_begin(view, y_in, z_in):
+        close = []
+        for k in [*range(1, z_count), 0]:
+            target = (z + k) % z_count
+            close.append(begin(view(target * 2 + 1 - y), y_in.at[k], near))
+        return SimpleNamespace(view=view, y_in=y_in, z_in=z_in, close=close, far=[], own=None)
+
+    def sum_step(state, index):
+        k = (index + 1) % z_count
+        state.close[index].wait_recv()
+        target = (z + k) % z_count
+        part = state.view(target * 2 + y)
+        total = wide(part[...]) + wide(state.y_in[k])
+        if k == 0:
+            state.own = total
+        else:
+            part[...] = low(total)
+            state.far.append(begin(part, state.z_in.at[k - 1], (target * 2 + y, s)))
+
+    def sum_middle(state):
+        for index in range(z_count):
+            sum_step(state, index)
+
+    def sum_end(state):
+        total = state.own
+        for k, copy in enumerate(state.far):
+            copy.wait_recv()
+            total = total + wide(state.z_in[k])
+        return total
+
+    cross, own = (c_query, c_key, c_value), (w_query, w_key, w_value)
+    up_wide = wide(w_up[...])
+    slab_out, slab_in = m.slab_out, m.slab_in
+    for j in range(seq_count):
+        full, half = 3 * (j // 2) + 2 * (j % 2), 3 * (j // 2) + 1
+        sources = [(matrix, full) for matrix in cross + own]
+        sources += [(matrix, half) for matrix in (cross if j % 2 == 0 else own)]
+        for k, (matrix, index) in enumerate(sources):
+            place = slice(LANES * k, LANES * k + LANES)
+            slab_out[j, :, place] = matrix[:, LANES * index : LANES * index + LANES]
+        for tile in range(hidden // LANES):
+            pieces = [
+                (up_wide, band * (seq_count * (at // band) + j) + at % band, at % LANES, size)
+                for at, size in spans(LANES * tile, LANES * tile + LANES, band)
+            ]
+            slab_out[j, :, 1152 + LANES * tile : 1152 + LANES * (tile + 1)] = low(
+                lane_pick(pieces, lane)
+            )
+    vec_own = m.vec_own
+    vec_own[...] = jnp.zeros(vec_own.shape, jnp.float32)
+    for k, ref in enumerate((b_down, *gains)):
+        vec_own[k : k + 1, 0:shard] = wide(ref[...])
+    vec_own[9:10, 0:band] = wide(b_up[...])
+    vec_all = m.vec_all
+    vec_all[d, s] = low(vec_own[...])
+    slab_in[s] = slab_out[s]
+    out_all, down_all, cot_all = m.out_all, m.down_all, m.cot_all
+    out_all[d, :, 0:width] = w_out[...]
+    out_all[d, :, width : 2 * width] = c_out[...]
+    down_all[block(d, band)] = w_down[...]
+    cot_all[block(s, tokens)] = cot[0]
+    m.rest_wide[...] = jnp.zeros(m.rest_wide.shape, jnp.float32)
+
+    def destination(index):
+        total = jnp.int32(0)
+        for k in range(slides):
+            total = total + jnp.where(slide[index] == k, owner[k], 0)
+        return total
+
+    own_places = [destination(d * tile_count + t) for t in range(tile_count)]
+    route = [
+        [jnp.where(place == p, 1.0, 0.0) for place in own_places] for p in range(data_count)
+    ]
+    spot = lax.broadcasted_iota(jnp.int32, (1, keys), 1)
+    slot_of = jnp.where(spot < keys_main, spot % inbox // main, (spot - keys_main) % data_count)
+    bias = jnp.zeros((1, keys), jnp.float32)
+    for p in range(data_count):
+        hits = jnp.int32(0)
+        for t in range(tile_count):
+            hits = hits + jnp.where(destination(p * tile_count + t) == d, 1, 0)
+        bias = jnp.where(slot_of == p, jnp.where(hits > 0, 0.0, MASKED_SCORE), bias)
+    m.key_bias[...] = bias
+    text_unit, _ = norm_parts(wide(text[0]))
+
+    pl.semaphore_wait(barrier, seq_count - 1 + data_count - 1)
+
+    own_vec = vec_all.at[d, s]
+    vec_seq = [begin(own_vec, own_vec, (d, peer)) for peer in seq_peers]
+    slab_seq = [begin(slab_out.at[peer], slab_in.at[s], (d, peer)) for peer in seq_peers]
+    tile_units = [norm_parts(wide(img[t]))[0] for t in range(tile_count)]
+    arrive(vec_seq)
+    vec_dp = [
+        begin(vec_all.at[d], vec_all.at[d], ((d + k) % data_count, s))
+        for k in range(1, data_count)
+    ]
+    arrive(slab_seq)
+    cols = m.cols
+    cols[block(d, band)] = low(
+        jnp.concatenate([wide(slab_in[j]) for j in range(seq_count)], axis=0)
+    )
+    self_view = lambda index: cols.at[block(index, band), lanes(384, 768)]
+    cross_view = lambda index: cols.at[block(index, band), lanes(0, 384)]
+    up_view = lambda index: cols.at[block(index, band), lanes(1152, hidden)]
+    down_view = lambda index: down_all.at[block(index, band)]
+    out_view = lambda index: out_all.at[index]
+    self_ag = gather_far(self_view)
+    gather_near(self_ag)
+    out_ag = gather_far(out_view)
+    gather_near(out_ag)
+
+    arrive(vec_dp)
+    stacked = vec_all[...].reshape(data_count * seq_count * 16, LANES)
+    row_of = lax.broadcasted_iota(jnp.int32, (LANES, width), 0)
+    col_of = lax.broadcasted_iota(jnp.int32, (LANES, width), 1)
+    spread = dot_plain(stacked, jnp.where(row_of == col_of % shard, 1.0, 0.0).astype(jnp.bfloat16))
+    spread = spread.reshape(data_count * seq_count, 16, width)
+    which = lax.broadcasted_iota(jnp.int32, spread.shape, 0)
+    column = lax.broadcasted_iota(jnp.int32, spread.shape, 2)
+    vec = m.vec
+    vec[...] = jnp.sum(jnp.where(which == column // shard, spread, 0.0), axis=0)
+
+    def vector(index):
+        return vec[index : index + 1, :]
+
+    h1, h2, h3, e1, e2 = m.h1, m.h2, m.h3, m.e1, m.e2
+    h1[block(s, tokens)] = low(text_unit * vector(1) + vector(2))
+    h1_ag = seq_gather(rows_of(h1))
+    cot_ag = seq_gather(rows_of(cot_all))
+
+    outbox, tiles = m.outbox, m.tiles
+    rest_rows, rest_wide, rest_out, rest_in = m.rest_rows, m.rest_wide, m.rest_out, m.rest_in
+    normed = [wide(low(unit * vector(5) + vector(6))) for unit in tile_units]
+    for p in range(data_count):
+        total = normed[0] * route[p][0]
+        for t in range(1, tile_count):
+            total = total + normed[t] * route[p][t]
+        outbox[block(p, main)] = low(total[0:main])
+        rest_rows[p : p + 1] = total[main:real_rows]
+    for k in range(columns):
+        rest_wide[pl.ds(k, data_count, stride=16), :] = rest_rows[:, LANES * k : LANES * (k + 1)]
+    rest_out[...] = low(rest_wide[0 : 16 * data_count]).reshape(rest_out.shape)
+    own_slot = block(s * data_count + d, main)
+    tiles[own_slot] = outbox[block(d, main)]
+    rest_in[s, d] = rest_out[d]
+
+    tile_dp = []
+
+    def tile_out(k):
+        peer = (d + k) % data_count
+        tile_dp.append(begin(outbox.at[block(peer, main)], tiles.at[own_slot], (peer, s)))
+        tile_dp.append(begin(rest_out.at[peer], rest_in.at[s, d], (peer, s)))
+
+    for k in range(2, data_count, 2):
+        tile_out(k)
+    seq_pass(h1_ag)
+    gather_forward(self_ag)
+    seq_pass(cot_ag)
+    gather_forward(out_ag)
+    for k in range(1, data_count, 2):
+        tile_out(k)
+    cross_ag = gather_far(cross_view)
+    up_ag = gather_far(up_view)
+    down_ag = gather_far(down_view)
+    gather_near(cross_ag)
+    gather_near(up_ag)
+    gather_near(down_ag)
+    gather_end(self_ag)
+    halves = m.halves
+    half_place = pl.ds(pl.multiple_of(core * 384, 384), 384)
+    half_copy = begin(cols.at[:, lanes(768, 384)], halves.at[:, half_place], (d, sibling))
+    halves[:, half_place] = cols[:, 768:1152]
+    seq_end(h1_ag)
+    qkv1, qm1, p1, o1 = m.qkv1, m.qm1, m.p1, m.o1
+    qkv1[:, 0:384] = low(dot_plain(h1[...], cols[:, 384:768]))
+    arrive([half_copy])
+    qkv1[:, 384:768] = low(dot_plain(h1[...], halves[:, 384:768]))
+
+    spot_q = lax.broadcasted_iota(jnp.int32, (length, length), 0)
+    spot_k = lax.broadcasted_iota(jnp.int32, (length, length), 1)
+    causal = spot_q >= spot_k
+    mixed = []
+    for head in range(3):
+        base = 384 * (head // 2)
+        qm = low(wide(qkv1[:, base : base + 128]) * head_masks[head])
+        qm1[block(head, length)] = qm
+        scores = dot_right(qm, qkv1[:, base + 128 : base + 256]) * factor
+        scores = jnp.where(causal, scores, MASKED_SCORE)
+        exponent = jnp.exp(scores - jnp.max(scores, axis=1, keepdims=True))
+        chances = exponent / jnp.sum(exponent, axis=1, keepdims=True)
+        p1[block(head, length)] = chances
+        mixed.append(
+            dot_plain(low(chances), qkv1[:, base + 256 : base + 384]) * head_masks[head]
+        )
+    o1[:, 0:128] = low(mixed[0] + mixed[1])
+    o1[:, 128:256] = low(mixed[2])
+
+    gather_end(out_ag)
+    per_seq = data_count // seq_count
+    out_in = m.out_in
+    out_seq = []
+    for peer in seq_peers:
+        out_seq.append(
+            begin(out_all.at[pl.ds(peer * per_seq, per_seq)], out_in.at[s], (d, peer))
+        )
+    out_in[s] = out_all[pl.ds(s * per_seq, per_seq)]
+    row_up = lax.broadcasted_iota(jnp.int32, (LANES, hidden), 0)
+    col_up = lax.broadcasted_iota(jnp.int32, (LANES, hidden), 1)
+    spread = dot_plain(stacked, jnp.where(row_up == col_up % band, 1.0, 0.0).astype(jnp.bfloat16))
+    spread = spread.reshape(data_count * seq_count, 16, hidden)
+    which = lax.broadcasted_iota(jnp.int32, spread.shape, 0)
+    column = lax.broadcasted_iota(jnp.int32, spread.shape, 2)
+    picked = jnp.where(which == (column // band) * seq_count + s, spread, 0.0)
+    m.up_bias[...] = jnp.sum(picked, axis=0)[9:10]
+
+    arrive(tile_dp)
+    whole_own = tiles.at[block(s, inbox)]
+    tile_pair = [
+        begin(whole_own, whole_own, (d, sibling)),
+        begin(rest_in.at[s], rest_in.at[s], (d, sibling)),
+    ]
+    rest_far = begin(rest_in.at[s], rest_in.at[s], (d, across))
+    quarter = inbox // 4
+
+    def quarter_of(index, k):
+        return tiles.at[pl.ds(pl.multiple_of(index * inbox + k * quarter, quarter), quarter)]
+
+    def tile_send(k):
+        part = quarter_of(s, k)
+        return begin(part, part, (d, across))
+
+    def tile_pass(k):
+        tile_far[k].wait_recv()
+        part = quarter_of(across, k)
+        tile_pair.append(begin(part, part, (d, sibling)))
+
+    tile_far = [tile_send(0)]
+    arrive(out_seq)
+    out_rows = m.out_rows
+    natural = jnp.concatenate(
+        [wide(out_in[j, i]) for i in range(per_seq) for j in range(seq_count)], axis=0
+    )
+    blank = jnp.zeros((64, 2 * width), jnp.float32)
+    even = jnp.concatenate([natural, blank], axis=0)
+    odd = jnp.concatenate([natural[64:192], blank, natural[0:64]], axis=0)
+    out_rows[...] = low(jnp.where(core == 0, even, odd))
+
+    state = seq_sum_begin(0, lambda i, j: dot_plain(pick(o1, i, j), out_rows[:, 0:width]))
+    state = seq_sum_pass(state)
+    tile_far.append(tile_send(1))
+    x2, x3, dx = m.x2, m.x3, m.dx
+    second = wide(text[0]) + seq_sum_end(state)
+    x2[...] = second
+    unit, _ = norm_parts(second)
+    h2[block(s, tokens)] = low(unit * vector(3) + vector(4))
+    h2_ag = seq_gather(rows_of(h2))
+    tile_far += [tile_send(2), tile_send(3)]
+
+    kv2, qm2, pr, o2, o_acc = m.kv2, m.qm2, m.pr, m.o2, m.o_acc
+
+    def keys_values(here):
+        rows = tiles[here]
+        kv2[here, 0:256] = low(dot_plain(rows, cols[:, 128:384]))
+        kv2[here, 256:512] = low(dot_plain(rows, halves[:, 128:384]))
+
+    gather_forward(cross_ag)
+    gather_end(cross_ag)
+    keys_values(block(s, inbox))
+    tile_pass(0)
+    seq_pass(h2_ag)
+    arrive(tile_pair[0:2])
+    keys_values(block(sibling, inbox))
+    tile_pass(1)
+    rest_far.wait_recv()
+    tile_pair.append(begin(rest_in.at[across], rest_in.at[across], (d, sibling)))
+    gather_step(up_ag, 0)
+    seq_end(h2_ag)
+    query_full = dot_plain(h2[...], cols[:, 0:128])
+    query_half = dot_plain(h2[...], halves[:, 0:128])
+    for head in range(3):
+        source = query_full if head < 2 else query_half
+        qm2[block(head, length)] = low(wide(low(source)) * head_masks[head])
+    tile_pass(2)
+    tile_pass(3)
+    keys_values(block(across, inbox))
+    arrive(tile_pair[2:])
+    keys_values(block(corner, inbox))
+    rest_wide[...] = wide(rest_in[...]).reshape(rest_wide.shape)
+    for k in range(columns):
+        tiles[keys_main:keys, LANES * k : LANES * (k + 1)] = low(
+            rest_wide[pl.ds(k, rests, stride=16), :]
+        )
+    keys_values(pl.ds(keys_main, rests))
+    gather_step(up_ag, 1)
+    gather_step(up_ag, 2)
+    for head in range(3):
+        base = 256 * (head // 2)
+        place = 128 * (head // 2)
+
+        @pl.loop(0, seq_count)
+        def _(i):
+            here = block(head * seq_count + i, tokens)
+            scores = dot_right(qm2[here], kv2[:, base : base + 128]) * factor + m.key_bias[...]
+            exponent = jnp.exp(scores - jnp.max(scores, axis=1, keepdims=True))
+            chances = low(exponent / jnp.sum(exponent, axis=1, keepdims=True))
+            pr[here] = chances
+            result = dot_plain(chances, kv2[:, base + 128 : base + 256]) * head_masks[head]
+            if head == 1:
+                result = result + o_acc[block(i, tokens), place : place + 128]
+            o_acc[block(i, tokens), place : place + 128] = result
+
+        if head < 2:
+            gather_step(down_ag, head)
+
+    o2[...] = low(o_acc[...])
+    state = seq_sum_begin(
+        1, lambda i, j: dot_plain(pick(o2, i, j), out_rows[:, width : 2 * width])
+    )
+    state = seq_sum_pass(state)
+    third = x2[...] + seq_sum_end(state)
+    x3[...] = third
+    unit, _ = norm_parts(third)
+    h3[block(s, tokens)] = low(unit * vector(7) + vector(8))
+    h3_ag = seq_gather(rows_of(h3))
+    seq_end(cot_ag)
+    seq_pass(h3_ag)
+    gather_step(down_ag, 2)
+    gather_end(down_ag)
+    act, slope, du = m.act, m.slope, m.du
+    slope[...] = dot_right(cot_all[...], down_all[...])
+    gather_end(up_ag)
+    seq_end(h3_ag)
+
+    @pl.loop(0, seq_count)
+    def _(i):
+        here = block(i, tokens)
+        pre = dot_plain(h3[here], cols[:, 1152 : 1152 + hidden]) + m.up_bias[...]
+        cdf = 0.5 * (1.0 + lax.erf(pre * (1.0 / math.sqrt(2.0))))
+        density = jnp.exp(-0.5 * pre * pre) * (1.0 / math.sqrt(2.0 * math.pi))
+        act[here] = low(pre * cdf)
+        grad = wide(low(slope[here]))
+        du[here] = low(grad * (cdf + pre * density))
+
+    state = seq_sum_begin(
+        2, lambda i, j: dot_right(pick(du, i, j), cols[:, 1152 : 1152 + hidden])
+    )
+    state = seq_sum_pass(state)
+    g_cols, g_down = m.g_cols, m.g_down
+    g_down[...] = low(dot_left(act[...], cot_all[...]))
+    g_down_view = lambda index: g_down.at[block(index, band)]
+    down_rs = sum_begin(g_down_view, m.y_down, m.z_down)
+    grad_mid = seq_sum_end(state)
+    unit, inverse = norm_parts(x3[...])
+    vv = m.vv
+    vv[...] = jnp.zeros(vv.shape, jnp.float32)
+    grad_out = wide(cot[0])
+    dx3 = grad_out + norm_back(unit, inverse, vector(7), grad_mid)
+    dx[...] = dx3
+    e2[block(s, tokens)] = low(dx3)
+    e2_ag = seq_gather(rows_of(e2))
+    vv[0:1] = column_sum(grad_out)
+    vv[7:8] = column_sum(grad_mid * unit)
+    vv[8:9] = column_sum(grad_mid)
+    vv[9:10, 0:hidden] = column_sum(wide(du[...]))
+
+    g_cols[:, 1152 : 1152 + hidden] = low(dot_left(h3[...], du[...]))
+    g_up_view = lambda index: g_cols.at[block(index, band), lanes(1152, hidden)]
+    up_rs = sum_begin(g_up_view, m.y_up, m.z_up)
+    sum_step(down_rs, 0)
+    seq_pass(e2_ag)
+    sum_step(down_rs, 1)
+    seq_end(e2_ag)
+
+    dom = m.dom
+    grad_o = low(dot_right(e2[...], out_rows[:, width : 2 * width]))
+    for head in range(3):
+        place = 128 * (head // 2)
+        dom[block(head, length)] = low(wide(grad_o[:, place : place + 128]) * head_masks[head])
+    ds, dkv2, dq2 = m.ds, m.dkv2, m.dq2
+    for head in range(3):
+        base = 256 * (head // 2)
+        place = 128 * (head // 2)
+
+        @pl.loop(0, seq_count)
+        def _(i):
+            here = block(head * seq_count + i, tokens)
+            chances = wide(pr[here])
+            grad_p = dot_right(dom[here], kv2[:, base + 128 : base + 256])
+            weighted = jnp.sum(chances * grad_p, axis=1, keepdims=True)
+            grad_s = low(chances * (grad_p - weighted))
+            ds[here] = grad_s
+            result = dot_plain(grad_s, kv2[:, base : base + 128]) * (head_masks[head] * factor)
+            if head == 1:
+                result = result + o_acc[block(i, tokens), place : place + 128]
+            o_acc[block(i, tokens), place : place + 128] = result
+
+        if head < 2:
+            sum_step(down_rs, 2 + head)
+
+    dq2[...] = low(o_acc[...])
+    state = seq_sum_begin(
+        4,
+        lambda i, j: dot_right(pick(dq2, i, j, slice(0, 128)), cols[:, 0:128])
+        + dot_right(pick(dq2, i, j, slice(128, 256)), halves[:, 0:128]),
+    )
+    state = seq_sum_pass(state)
+
+    g_out, g_out_send = m.g_out, m.g_out_send
+
+    def out_grad(slot, value):
+        odd = jnp.concatenate([value[192:256], value[0:128]], axis=0)
+        natural = jnp.where(core == 0, value[0:192], odd)
+        for i in range(per_seq):
+            for j in range(seq_count):
+                start = shard * (i * seq_count + j)
+                g_out_send[slot, j, i] = low(natural[start : start + shard])
+        target = g_out.at[pl.ds(s * per_seq, per_seq), :, lanes(slot * width, width)]
+        copies = [begin(g_out_send.at[slot, peer], target, (d, peer)) for peer in seq_peers]
+        g_out[pl.ds(s * per_seq, per_seq), :, slot * width : (slot + 1) * width] = g_out_send[
+            slot, s
+        ]
+        return copies
+
+    xout_seq = out_grad(1, dot_left(o2[...], e2[...]))
+    sum_step(up_rs, 0)
+    second_grad = seq_sum_end(state)
+    unit, inverse = norm_parts(x2[...])
+    dx2 = dx[...] + norm_back(unit, inverse, vector(3), second_grad)
+    dx[...] = dx2
+    e1[block(s, tokens)] = low(dx2)
+    e1_ag = seq_gather(rows_of(e1))
+    vv[3:4] = column_sum(second_grad * unit)
+    vv[4:5] = column_sum(second_grad)
+    sum_step(up_rs, 1)
+    arrive(xout_seq)
+    xout_view = lambda index: g_out.at[index, :, lanes(width, width)]
+    xout_rs = sum_begin(xout_view, m.y_xout, m.z_xout)
+
+    for tile in range(2):
+        first, count = (0, 2 * length) if tile == 0 else (2 * length, length)
+        base = 256 * tile
+        for start, size in spans(0, keys, 512):
+            cut = slice(start, start + size)
+            dkv2[cut, base : base + 128] = low(
+                dot_left(ds[first : first + count, cut], qm2[first : first + count]) * factor
+            )
+            dkv2[cut, base + 128 : base + 256] = low(
+                dot_left(pr[first : first + count, cut], dom[first : first + count])
+            )
+    seq_pass(e1_ag)
+    sum_step(up_rs, 2)
+    dn = m.dn
+
+    def tile_grads(here):
+        dn[here] = low(
+            dot_right(dkv2[here, 0:256], cols[:, 128:384])
+            + dot_right(dkv2[here, 256:512], halves[:, 128:384])
+        )
+
+    dr_out, dr_pair, dr_far, dr_home = m.dr_out, m.dr_pair, m.dr_far, m.dr_home
+    dn_pair, dn_far, dn_home = m.dn_pair, m.dn_far, m.dn_home
+    tile_grads(block(corner, inbox))
+    pair_far = begin(dn.at[block(corner, inbox)], dn_pair.at[1], (d, sibling))
+    tile_grads(pl.ds(keys_main, rests))
+    rest_wide[...] = jnp.zeros(rest_wide.shape, jnp.float32)
+    for k in range(columns):
+        rest_wide[pl.ds(k, rests, stride=16), :] = wide(
+            dn[keys_main:keys, LANES * k : LANES * (k + 1)]
+        )
+    dr_out[...] = low(rest_wide[...]).reshape(dr_out.shape)
+    rest_pair = [
+        begin(dr_out.at[peer], dr_pair.at[k], (d, sibling))
+        for k, peer in enumerate((sibling, corner))
+    ]
+    tile_grads(block(across, inbox))
+    pair_far.wait_recv()
+    fold = dn.at[block(across, inbox)]
+    fold[...] = low(wide(fold[...]) + wide(dn_pair[1]))
+    arrive(rest_pair)
+    dr_out[across] = low(wide(dr_out[across]) + wide(dr_pair[1]))
+    rest_far = begin(dr_out.at[across], dr_far, (d, across))
+
+    def far_send(k):
+        return begin(quarter_in(dn, across, k), dn_far.at[block(k, quarter)], (d, across))
+
+    def quarter_in(ref, index, k):
+        return ref.at[pl.ds(pl.multiple_of(index * inbox + k * quarter, quarter), quarter)]
+
+    far_copies = [far_send(0)]
+    g_half, g_half2, half_in = m.g_half, m.g_half2, m.half_in
+    grad = dot_left(h2[...], dq2[...])
+    g_cols[:, 0:128] = low(grad[:, 0:128])
+    g_half[:, 0:128] = low(grad[:, 128:256])
+    for cut in range(3):
+        span = slice(256 * cut, 256 * cut + 256)
+        grad = dot_left(tiles[:, span], dkv2[...])
+        g_cols[span, 128:384] = low(grad[:, 0:256])
+        g_half[span, 128:384] = low(grad[:, 256:512])
+    half_cross = links.make(g_half, half_in, (d, sibling))
+
+    @pl.when(core == 1)
+    def _():
+        half_cross.start()
+
+    g_cross_view = lambda index: g_cols.at[block(index, band), lanes(0, 384)]
+    cross_rs = sum_begin(g_cross_view, m.y_cross, m.z_cross)
+    far_copies += [far_send(1)]
+    tile_grads(block(sibling, inbox))
+    pair_own = begin(dn.at[block(sibling, inbox)], dn_pair.at[0], (d, sibling))
+    tile_grads(block(s, inbox))
+    sum_step(up_rs, 3)
+    sum_middle(xout_rs)
+
+    seq_end(e1_ag)
+    grad_o = low(dot_right(e1[...], out_rows[:, 0:width]))
+    grads = []
+    dqkv = m.dqkv
+    for head in range(3):
+        base = 384 * (head // 2)
+        place = 128 * (head // 2)
+        here = block(head, length)
+        dm = low(wide(grad_o[:, place : place + 128]) * head_masks[head])
+        chances = p1[here]
+        grad_p = dot_right(dm, qkv1[:, base + 256 : base + 384])
+        weighted = jnp.sum(chances * grad_p, axis=1, keepdims=True)
+        grad_s = low(chances * (grad_p - weighted))
+        grads.append(
+            (
+                dot_plain(grad_s, qkv1[:, base + 128 : base + 256]) * (head_masks[head] * factor),
+                dot_left(grad_s, qm1[here]) * factor,
+                dot_left(low(chances), dm),
+            )
+        )
+    for k in range(3):
+        dqkv[:, 128 * k : 128 * k + 128] = low(grads[0][k] + grads[1][k])
+        dqkv[:, 384 + 128 * k : 512 + 128 * k] = low(grads[2][k])
+    state = seq_sum_begin(
+        5,
+        lambda i, j: dot_right(pick(dqkv, i, j, slice(0, 384)), cols[:, 384:768])
+        + dot_right(pick(dqkv, i, j, slice(384, 768)), halves[:, 384:768]),
+    )
+
+    grad = dot_left(h1[...], dqkv[...])
+    g_cols[:, 384:768] = low(grad[:, 0:384])
+    g_half2[...] = low(grad[:, 384:768])
+    half_self = links.make(g_half2, half_in, (d, sibling))
+
+    @pl.when(core == 0)
+    def _():
+        half_self.start()
+
+    state = seq_sum_pass(state)
+    sout_seq = out_grad(0, dot_left(o1[...], e1[...]))
+    far_copies += [far_send(2), far_send(3)]
+    g_self_view = lambda index: g_cols.at[block(index, band), lanes(384, 768)]
+
+    @pl.when(core == 0)
+    def _():
+        half_cross.wait_recv()
+        g_cols[:, 768:1152] = low(wide(g_half[...]) + wide(half_in[...]))
+
+    @pl.when(core == 1)
+    def _():
+        half_self.wait_recv()
+        g_cols[:, 768:1152] = low(wide(g_half2[...]) + wide(half_in[...]))
+
+    self_rs = sum_begin(g_self_view, m.y_self, m.z_self)
+    arrive(sout_seq)
+    sout_view = lambda index: g_out.at[index, :, lanes(0, width)]
+    sout_rs = sum_begin(sout_view, m.y_sout, m.z_sout)
+    sum_middle(cross_rs)
+
+    arrive([pair_own, rest_far])
+    dr_out[s] = low(wide(dr_out[s]) + wide(dr_pair[0]) + wide(dr_far[...]))
+    for k in range(4):
+        far_copies[k].wait_recv()
+        mine = quarter_in(dn, s, k)
+        there = block(k, quarter)
+        mine[...] = low(wide(mine[...]) + wide(dn_pair[0, there]) + wide(dn_far[there]))
+    home_dp = []
+    own_home = block(d, main)
+    for k in range(1, data_count):
+        peer = (d + k) % data_count
+        source = dn.at[block(s * data_count + peer, main)]
+        home_dp.append(begin(source, dn_home.at[own_home], (peer, s)))
+        home_dp.append(begin(dr_out.at[s, peer], dr_home.at[d], (peer, s)))
+    dn_home[own_home] = dn[block(s * data_count + d, main)]
+    dr_home[d] = dr_out[s, d]
+
+    first_grad = seq_sum_end(state)
+    unit, inverse = norm_parts(wide(text[0]))
+    vv[1:2] = column_sum(first_grad * unit)
+    vv[2:3] = column_sum(first_grad)
+    r_tgrad[...] = low(dx[...] + norm_back(unit, inverse, vector(1), first_grad))
+    out_state = seq_sum_begin(3, lambda i, j: dot_plain(pick(act, i, j), down_all[...]))
+    out_state = seq_sum_pass(out_state)
+
+    sum_middle(self_rs)
+    sum_middle(sout_rs)
+    r_text[...] = low(x3[...] + seq_sum_end(out_state) + vector(0))
+
+    cols_out, cols_in = m.cols_out, m.cols_in
+
+    def finish_cols(first, size, state):
+        total = low(sum_end(state))
+        place = lanes(first, size)
+        total = wide(total)
+        for j in range(seq_count):
+            cols_out[j, :, place] = low(total[shard * j : shard * (j + 1)])
+        cols_in[s, :, place] = cols_out[s, :, place]
+        return [
+            begin(cols_out.at[peer, :, place], cols_in.at[s, :, place], (d, peer))
+            for peer in seq_peers
+        ]
+
+    r_down[...] = sum_end(down_rs)
+    ends = finish_cols(1152, hidden, up_rs)
+    r_outs[1] = sum_end(xout_rs)
+    ends += finish_cols(0, 384, cross_rs)
+
+    arrive(home_dp)
+    gain_sum = jnp.zeros((1, width), jnp.float32)
+    shift_sum = jnp.zeros((1, width), jnp.float32)
+    for t in range(tile_count):
+        grad = wide(dn_home[block(0, main)]) * route[0][t]
+        rest = wide(dr_home[0]) * route[0][t]
+        for p in range(1, data_count):
+            grad = grad + wide(dn_home[block(p, main)]) * route[p][t]
+            rest = rest + wide(dr_home[p]) * route[p][t]
+        rest = jnp.concatenate([rest[k : k + 1] for k in range(columns)], axis=1)
+        unit, inverse = norm_parts(wide(img[t, 0:main]))
+        gain_sum = gain_sum + column_sum(grad * unit)
+        shift_sum = shift_sum + column_sum(grad)
+        r_igrad[t, 0:main] = low(norm_back(unit, inverse, vector(5), grad))
+        unit, inverse = norm_parts(wide(img[t, main:real_rows]))
+        gain_sum = gain_sum + rest * unit
+        shift_sum = shift_sum + rest
+        r_igrad[t, main:real_rows] = low(norm_back(unit, inverse, vector(5), rest))
+    vv[5:6] = gain_sum
+    vv[6:7] = shift_sum
+
+    vv_out, vv_in, vq = m.vv_out, m.vv_in, m.vq
+    everything = vv[...]
+    for p in range(data_count):
+        turned = everything if p == 0 else pltpu.roll(everything, width - band * p, 1)
+        vv_out[p] = turned[:, 0:LANES]
+    vv_dp = []
+    for k in range(1, data_count):
+        peer = (d + k) % data_count
+        vv_dp.append(begin(vv_out.at[peer], vv_in.at[d], (peer, s)))
+    vv_in[d] = vv_out[d]
+
+    ends += finish_cols(384, 768, self_rs)
+    r_outs[0] = sum_end(sout_rs)
+
+    arrive(vv_dp)
+    total = vv_in[0]
+    for p in range(1, data_count):
+        total = total + vv_in[p]
+    vq[s] = total
+    vq_seq = [begin(vq.at[s], vq.at[s], (d, peer)) for peer in seq_peers]
+    bias_grad = total[9:10]
+
+    arrive(ends)
+    r_cols[...] = cols_in[...]
+    arrive(vq_seq)
+    total = vq[0] + vq[1] + vq[2] + vq[3]
+    r_vec[...] = pltpu.roll(total, (LANES - shard * s) % LANES, 1)
+    r_vec[9:10] = bias_grad
+
+    for copy in links.started:
+        copy.wait_send()
+
+    @pl.when(core == 0)
+    def _():
+        half_self.wait_send()
+
+    @pl.when(core == 1)
+    def _():
+        half_cross.wait_send()
+
+
+def unpack_kernel(t_out, t_grad, i_grad, cols, outs, down, vec, *results):
+    o_text, o_tgrad, o_igrad, o_q, o_k, o_v, o_o, o_xq, o_xk, o_xv, o_xo, o_up, o_down, *vectors = (
+        results
+    )
+    seq_count, shard, total = cols.shape
+    hidden = total - 1152
+    band = down.shape[0]
+    o_text[0] = t_out[...]
+    o_tgrad[0] = t_grad[...]
+    o_igrad[...] = i_grad[...]
+    for k, result in enumerate((o_xq, o_xk, o_xv, o_q, o_k, o_v)):
+        here = slice(LANES * k, LANES * (k + 1))
+        there = slice(768 + LANES * (k % 3), 768 + LANES * (k % 3 + 1))
+        carrier = k // 3
+        for j, tile in ((0, 0), (1, 2), (2, 3), (3, 5)):
+            result[:, LANES * tile : LANES * (tile + 1)] = wide(cols[j, :, here])
+        for j, tile in ((carrier, 1), (2 + carrier, 4)):
+            result[:, LANES * tile : LANES * (tile + 1)] = wide(cols[j, :, there])
+    o_o[...] = outs[0]
+    o_xo[...] = outs[1]
+    o_down[...] = down[...]
+    lane = lax.broadcasted_iota(jnp.int32, (1, LANES), 1)
+    parts = [wide(cols[j, :, 1152:total]) for j in range(seq_count)]
+    for tile in range(hidden * seq_count // LANES):
+        pieces = []
+        for at, size in spans(LANES * tile, LANES * tile + LANES, band):
+            group = at // band
+            first = band * (group // seq_count) + at % band
+            pieces.append((parts[group % seq_count], first, at % LANES, size))
+        o_up[:, LANES * tile : LANES * (tile + 1)] = lane_pick(pieces, lane)
+    vectors[0][...] = vec[9, 0:band]
+    for k, result in enumerate(vectors[1:]):
+        result[...] = vec[k, 0:shard]
+
+
+def fused_device(
+    text_in, image_in, tile_slide, owner_map, text_cot,
+    w_query, w_key, w_value, w_out, c_query, c_key, c_value, c_out, w_up, w_down, b_up, b_down,
+    self_gain, self_shift, cross_gain, cross_shift, tile_gain, tile_shift, mlp_gain, mlp_shift,
+):
+    data_count, seq_count = lax.axis_size("dp"), lax.axis_size("seq")
+    tile_count, real_rows, width = image_in.shape
+    tokens = text_in.shape[1]
+    shard = w_query.shape[0]
+    band = shard * seq_count
+    hidden = w_up.shape[1] // seq_count
+    main = real_rows // 16 * 16
+
+    gains = (
+        self_gain, self_shift, cross_gain, cross_shift, tile_gain, tile_shift, mlp_gain, mlp_shift,
+    )
+    inputs = (
+        tile_slide, owner_map, text_in, image_in, text_cot, w_query, w_key, w_value, w_out,
+        c_query, c_key, c_value, c_out, w_up, w_down,
+        *[member.reshape(1, -1) for member in (b_up, b_down, *gains)],
+    )
+    in_specs = [pl.BlockSpec(memory_space=pltpu.SMEM)] * 2
+    in_specs += [pl.BlockSpec(memory_space=pltpu.VMEM)] * (len(inputs) - 2)
+    row_out = jax.ShapeDtypeStruct((tokens, width), jnp.bfloat16)
+    packed_shape = [
+        row_out,
+        row_out,
+        jax.ShapeDtypeStruct(image_in.shape, jnp.bfloat16),
+        jax.ShapeDtypeStruct((seq_count, shard, 1152 + hidden), jnp.bfloat16),
+        jax.ShapeDtypeStruct((2, shard, width), jnp.float32),
+        jax.ShapeDtypeStruct((band, width), jnp.float32),
+        jax.ShapeDtypeStruct((16, LANES), jnp.float32),
+    ]
+    shapes = scratch_of(width, tokens, seq_count, data_count, hidden, main, shard)
+    scratch = [pltpu.VMEM(shape, kind) for shape, kind in shapes.values()]
+    scratch += [pltpu.SemaphoreType.DMA((COPY_SLOTS,))] * 2
+    names = [*shapes, "send", "recv"]
+    packed = pl.pallas_call(
+        partial(fused_kernel, names, len(inputs)),
+        out_shape=packed_shape,
+        in_specs=in_specs,
+        out_specs=[pl.BlockSpec(memory_space=pltpu.VMEM)] * len(packed_shape),
+        scratch_shapes=scratch,
+        compiler_params=pltpu.CompilerParams(
+            collective_id=0, has_side_effects=True, vmem_limit_bytes=60 * 1024 * 1024
+        ),
+        name="decoder_layer",
+    )(*inputs)
+    square = jax.ShapeDtypeStruct((shard, width), jnp.float32)
+    out_shape = [
+        jax.ShapeDtypeStruct(text_in.shape, jnp.bfloat16),
+        jax.ShapeDtypeStruct(text_in.shape, jnp.bfloat16),
+        jax.ShapeDtypeStruct(image_in.shape, jnp.bfloat16),
+        *[square] * 8,
+        jax.ShapeDtypeStruct((shard, hidden * seq_count), jnp.float32),
+        jax.ShapeDtypeStruct((band, width), jnp.float32),
+        jax.ShapeDtypeStruct((band,), jnp.float32),
+        *[jax.ShapeDtypeStruct((shard,), jnp.float32)] * 9,
+    ]
+    return tuple(
+        pl.pallas_call(
+            unpack_kernel,
+            out_shape=out_shape,
+            in_specs=[pl.BlockSpec(memory_space=pltpu.VMEM)] * len(packed),
+            out_specs=[pl.BlockSpec(memory_space=pltpu.VMEM)] * len(out_shape),
+            name="unpack",
+        )(*packed)
+    )
+
+
+def fused_fits(mesh):
+    return mesh.shape["seq"] == 4 and 768 % (8 * mesh.shape["dp"] * mesh.shape["seq"]) == 0
+
+
 def solution(mesh):
     placed = (
         P("dp", "seq", None),
@@ -557,7 +1671,7 @@
         P(("dp", "seq")),
     )
     return jax.shard_map(
-        per_device,
+        fused_device if fused_fits(mesh) else per_device,
         mesh=mesh,
         in_specs=placed,
         out_specs=(

time: 1510 us -> 199 us (0.13); the launches traced: 1490 us -> 199 us
  waiting for transfers between devices: 981 us -> 0 us
  blocking collectives: 208 us -> 0 us
  Pallas kernels: 0 us -> 195 us
  local copies, waits for them, and re-layouts: 122 us -> 3.53 us
  matrix products: 86.2 us -> 0 us
  starting transfers between devices: 44.3 us -> 0 us
  other arithmetic: 33.6 us -> 0 us
  between operations: 16.3 us -> 0.67 us
    all_gather x10 -> x0, waiting for transfers between devices: 424 us -> none  [the longest x1 64.4 us: per_device(): lax.all_gather(w_up, ('dp', 'seq'), axis=0, tiled=True)]
    reduce_scatter x10 -> x0, waiting for transfers between devices: 346 us -> none  [the longest x1 72.2 us: per_device(): lax.psum_scatter(folded[8], 'dp', scatter_dimension=0, tiled=True)]
    pallas_call x0 -> x2, Pallas kernels: none -> 195 us  [the longest x1 192 us: fused_device(): pl.pallas_call(partial(fused_kernel, names, len(inputs)), out_shape=packe...]
    all_to_all x10 -> x0, waiting for transfers between devices: 162 us -> none  [the longest x1 47.9 us: per_device(): lax.all_to_all(split_rows(up_grad, data_count, seq_count).astype(jnp.bflo...]
    dot_general x128 -> x0, matrix products: 86.2 us -> none  [the longest x10 26 us: matmul(): return jnp.dot(former, latter, preferred_element_type=jnp.float32)]
    unnamed x2 -> x0, blocking collectives: 81.8 us -> none
    all_to_all x2 -> x0, blocking collectives: 76.1 us -> none  [the longest x1 56.4 us: per_device(): lax.all_to_all(split_rows(down_grad, data_count, seq_count).astype(jnp.bf...]
    unnamed x28 -> x0, waiting for transfers between devices: 48.5 us -> none
  transfers between devices with their start and end apart: 34 -> 0, of which waited for: 27 -> 0; matrix products, arithmetic and copies ran while one was open for 8% -> 0% of each run, Pallas kernels for 0% -> 0%
where the time goes in v1:
time: 199 us
  Pallas kernels  195 us (98%)
  local copies, waits for them, and re-layouts  3.53 us (2%)
    pallas_call x1, Pallas kernels, fused_device(): pl.pallas_call(partial(fused_kernel, names, len(inputs)), out_shape=packe...  192 us

profile of v1, /device:TPU:0, one launch (start us, length us, event | category | flops | bytes accessed | tf_op | source)
XLA Modules:
  0.0 199.0 jit_solution(7708633015386595407)
XLA Ops:
  0.7 1.7 copy.48.refs_3_
  2.4 192.1 %decoder_layer.1 = (bf16[64,768]{1,0:T(8,128)(2,1)}, bf16[64,768]{1,0:T(8,128)(2,1)}, bf16[4,49,768]{2,1,0:T(8,128)(2,1)}, bf16[4,24,1920]{2,1,0:T(8,128)(2,1)},...) custom-call(s32[32]{0:T(128)} %refs_0_.1, s32[8]{0:T(128)} %refs_1_.1, bf16[1,64,768]{2,1,0:T(8,128)(2,1)} %refs_2_.1, ...), custom_call_target="tpu_custom_call" | custom-call | tf_op jit(solution)/shard_map/decoder_layer/pallas_call | solution.py:1608
  194.5 2.6 %unpack.1 = (bf16[1,64,768]{2,1,0:T(8,128)(2,1)}, bf16[1,64,768]{2,1,0:T(8,128)(2,1)}, bf16[4,49,768]{2,1,0:T(8,128)(2,1)}, f32[24,768]{1,0:T(8,128)}, f32[24,76...) custom-call(bf16[64,768]{1,0:T(8,128)(2,1)} %get-tuple-element.30.t_, ...), custom_call_target="tpu_custom_call" | custom-call | tf_op jit(solution)/shard_map/unpack/pallas_call | solution.py:1631
  197.1 1.8 copy.49

commit v2 on v1

--- a/solution.py
+++ b/solution.py
@@ -627,10 +627,10 @@
         vec=((16, width), f32),
         up_bias=((1, hidden), f32),
         key_bias=((1, keys), f32),
-        slab_out=((seq_count, shard, 1152 + hidden), bf16),
-        slab_in=((seq_count, shard, 1152 + hidden), bf16),
-        cols=((width, 1152 + hidden), bf16),
-        halves=((width, 768), bf16),
+        slab_out=((seq_count, shard, 1536 + hidden), bf16),
+        slab_in=((seq_count, shard, 1536 + hidden), bf16),
+        cols=((width, 768 + hidden), bf16),
+        halves=((data_count, 2, band // 2, 768), bf16),
         cot_all=((length, width), bf16),
         h1=((length, width), bf16),
         h2=((length, width), bf16),
@@ -677,10 +677,10 @@
         dr_pair=((2, data_count, 16, LANES), bf16),
         dr_far=((data_count, 16, LANES), bf16),
         dr_home=((data_count, 16, LANES), bf16),
-        g_cols=((width, 1152 + hidden), bf16),
-        g_half=((width, 384), bf16),
-        g_half2=((width, 384), bf16),
-        half_in=((width, 384), bf16),
+        g_cols=((width, 768 + hidden), bf16),
+        g_half=((data_count, 2, band // 2, 768), bf16),
+        half_in=((data_count, band // 2, 768), bf16),
+        g_cross=((width, 256), bf16),
         g_down=((hidden, width), bf16),
         g_out=((data_count, shard, 2 * width), bf16),
         g_out_send=((2, seq_count, data_count // seq_count, shard, width), bf16),
@@ -688,16 +688,18 @@
         z_up=((3, band, hidden), bf16),
         y_down=((4, band, width), bf16),
         z_down=((3, band, width), bf16),
-        y_cross=((4, band, 384), bf16),
-        z_cross=((3, band, 384), bf16),
-        y_self=((4, band, 768), bf16),
-        z_self=((3, band, 768), bf16),
+        y_full=((4, band, 768), bf16),
+        z_full=((3, band, 768), bf16),
+        y_half=((4, band // 2, 768), bf16),
+        z_half=((3, band // 2, 768), bf16),
         y_xout=((4, shard, width), bf16),
         z_xout=((3, shard, width), bf16),
         y_sout=((4, shard, width), bf16),
         z_sout=((3, shard, width), bf16),
-        cols_out=((seq_count, shard, 1152 + hidden), bf16),
-        cols_in=((seq_count, shard, 1152 + hidden), bf16),
+        cols_out=((seq_count, shard, 768 + hidden), bf16),
+        cols_in=((seq_count, shard, 768 + hidden), bf16),
+        ends_out=((2, shard, 768), bf16),
+        ends_in=((seq_count, shard, 768), bf16),
         vv=((16, width), f32),
         vv_out=((data_count, 16, LANES), f32),
         vv_in=((data_count, 16, LANES), f32),
@@ -734,8 +736,8 @@
         slide, owner, text, img, cot, w_query, w_key, w_value, w_out, c_query, c_key, c_value,
         c_out, w_up, w_down, b_up, b_down, *gains,
     ) = refs[:n_in]
-    r_text, r_tgrad, r_igrad, r_cols, r_outs, r_down, r_vec = refs[n_in : n_in + 7]
-    m = SimpleNamespace(**dict(zip(names, refs[n_in + 7 :])))
+    r_text, r_tgrad, r_igrad, r_cols, r_half, r_outs, r_down, r_vec = refs[n_in : n_in + 8]
+    m = SimpleNamespace(**dict(zip(names, refs[n_in + 8 :])))
     links = Copies(m.send, m.recv)
     begin = links.begin
 
@@ -765,9 +767,12 @@
     across = (s + 2) % 4
     corner = 3 - s
     seq_peers = [sibling, across, corner]
-    z_peers = [(z + k) % z_count for k in range(1, z_count)]
-    z_from = [(z + z_count - k) % z_count for k in range(1, z_count)]
+    z_pair = z + 1 - 2 * (z % 2)
+    z_across = (z + 2) % 4
+    z_corner = 3 - z
     near = (z * 2 + 1 - y, s)
+    beside = (z_pair * 2 + y, s)
+    beyond = (z_across * 2 + y, s)
 
     barrier = pltpu.get_barrier_semaphore()
     for peer in seq_peers:
@@ -805,23 +810,23 @@
     def rows_of(ref):
         return [lambda index: ref.at[block(index, tokens)]]
 
+    def send_all(refs, device):
+        return [begin(ref, ref, device) for ref in refs]
+
     def gather_far(view):
         own = view(d)
-        return view, [begin(own, own, (peer * 2 + y, s)) for peer in z_peers], []
+        return view, [send_all(own, beyond), send_all(own, beside)], []
 
     def gather_near(state):
-        own = state[0](d)
-        state[2].append(begin(own, own, near))
+        state[2].extend(send_all(state[0](d), near))
 
     def gather_step(state, k):
         view, far, close = state
-        far[k].wait_recv()
-        part = view(z_from[k] * 2 + y)
-        close.append(begin(part, part, near))
-
-    def gather_forward(state):
-        for k in range(z_count - 1):
-            gather_step(state, k)
+        arrive(far[k])
+        part = view((z_across, z_pair, z_corner)[k] * 2 + y)
+        if k == 0:
+            far.append(send_all(part, beside))
+        close.extend(send_all(part, near))
 
     def gather_end(state):
         arrive(state[2])
@@ -852,35 +857,45 @@
             [ref[block(first, tokens), place], ref[block(second, tokens), place]], axis=0
         )
 
+    sum_targets = (z_corner, z_pair, z_across, z)
+
     def sum_begin(view, y_in, z_in):
-        close = []
-        for k in [*range(1, z_count), 0]:
-            target = (z + k) % z_count
-            close.append(begin(view(target * 2 + 1 - y), y_in.at[k], near))
-        return SimpleNamespace(view=view, y_in=y_in, z_in=z_in, close=close, far=[], own=None)
-
-    def sum_step(state, index):
-        k = (index + 1) % z_count
-        state.close[index].wait_recv()
-        target = (z + k) % z_count
-        part = state.view(target * 2 + y)
-        total = wide(part[...]) + wide(state.y_in[k])
-        if k == 0:
-            state.own = total
-        else:
+        close = [
+            [
+                begin(part, ref.at[k], near)
+                for part, ref in zip(view(target * 2 + 1 - y), y_in, strict=True)
+            ]
+            for k, target in enumerate(sum_targets)
+        ]
+        return SimpleNamespace(view=view, y_in=y_in, z_in=z_in, close=close, far=[], own=[])
+
+    def sum_step(state, k):
+        arrive(state.close[k])
+        if k == 2:
+            arrive(state.far[0])
+        copies = []
+        for index, part in enumerate(state.view(sum_targets[k] * 2 + y)):
+            total = wide(part[...]) + wide(state.y_in[index][k])
+            if k == 3:
+                state.own.append(total)
+                continue
+            if k == 2:
+                total = total + wide(state.z_in[index][0])
             part[...] = low(total)
-            state.far.append(begin(part, state.z_in.at[k - 1], (target * 2 + y, s)))
+            target = state.z_in[index].at[k]
+            copies.append(begin(part, target, beyond if k == 2 else beside))
+        state.far.append(copies)
 
     def sum_middle(state):
-        for index in range(z_count):
-            sum_step(state, index)
+        for k in range(4):
+            sum_step(state, k)
 
     def sum_end(state):
-        total = state.own
-        for k, copy in enumerate(state.far):
-            copy.wait_recv()
-            total = total + wide(state.z_in[k])
-        return total
+        arrive(state.far[1] + state.far[2])
+        return [
+            own + wide(ref[1]) + wide(ref[2])
+            for own, ref in zip(state.own, state.z_in, strict=True)
+        ]
 
     cross, own = (c_query, c_key, c_value), (w_query, w_key, w_value)
     up_wide = wide(w_up[...])
@@ -888,7 +903,7 @@
     for j in range(seq_count):
         full, half = 3 * (j // 2) + 2 * (j % 2), 3 * (j // 2) + 1
         sources = [(matrix, full) for matrix in cross + own]
-        sources += [(matrix, half) for matrix in (cross if j % 2 == 0 else own)]
+        sources += [(matrix, half) for matrix in cross + own]
         for k, (matrix, index) in enumerate(sources):
             place = slice(LANES * k, LANES * k + LANES)
             slab_out[j, :, place] = matrix[:, LANES * index : LANES * index + LANES]
@@ -897,7 +912,7 @@
                 (up_wide, band * (seq_count * (at // band) + j) + at % band, at % LANES, size)
                 for at, size in spans(LANES * tile, LANES * tile + LANES, band)
             ]
-            slab_out[j, :, 1152 + LANES * tile : 1152 + LANES * (tile + 1)] = low(
+            slab_out[j, :, 1536 + LANES * tile : 1536 + LANES * (tile + 1)] = low(
                 lane_pick(pieces, lane)
             )
     vec_own = m.vec_own
@@ -936,33 +951,73 @@
     m.key_bias[...] = bias
     text_unit, _ = norm_parts(wide(text[0]))
 
+    outbox, tiles = m.outbox, m.tiles
+    rest_rows, rest_wide, rest_out, rest_in = m.rest_rows, m.rest_wide, m.rest_out, m.rest_in
+    units = [wide(low(norm_parts(wide(img[t]))[0])) for t in range(tile_count)]
+    for p in range(data_count):
+        total = units[0] * route[p][0]
+        for t in range(1, tile_count):
+            total = total + units[t] * route[p][t]
+        outbox[block(p, main)] = low(total[0:main])
+        rest_rows[p : p + 1] = total[main:real_rows]
+    for k in range(columns):
+        rest_wide[pl.ds(k, data_count, stride=16), :] = rest_rows[:, LANES * k : LANES * (k + 1)]
+    rest_out[...] = low(rest_wide[0 : 16 * data_count]).reshape(rest_out.shape)
+    own_slot = block(s * data_count + d, main)
+    tiles[own_slot] = outbox[block(d, main)]
+    rest_in[s, d] = rest_out[d]
+    tile_dp = []
+
+    def tile_out(k):
+        peer = (d + k) % data_count
+        tile_dp.append(begin(outbox.at[block(peer, main)], tiles.at[own_slot], (peer, s)))
+        tile_dp.append(begin(rest_out.at[peer], rest_in.at[s, d], (peer, s)))
+
     pl.semaphore_wait(barrier, seq_count - 1 + data_count - 1)
 
     own_vec = vec_all.at[d, s]
-    vec_seq = [begin(own_vec, own_vec, (d, peer)) for peer in seq_peers]
+    vec_dp = [begin(own_vec, own_vec, ((d + k) % data_count, s)) for k in range(1, data_count)]
     slab_seq = [begin(slab_out.at[peer], slab_in.at[s], (d, peer)) for peer in seq_peers]
-    tile_units = [norm_parts(wide(img[t]))[0] for t in range(tile_count)]
-    arrive(vec_seq)
-    vec_dp = [
-        begin(vec_all.at[d], vec_all.at[d], ((d + k) % data_count, s))
-        for k in range(1, data_count)
-    ]
+    for k in (2, 1, 4, 3, 6, 5, 7):
+        tile_out(k)
+    out_view = lambda index: [out_all.at[index]]
+    out_ag = gather_far(out_view)
+    gather_near(out_ag)
+    arrive(vec_dp)
+    vec_column = vec_all.at[:, s]
+    vec_seq = [begin(vec_column, vec_column, (d, peer)) for peer in seq_peers]
     arrive(slab_seq)
-    cols = m.cols
-    cols[block(d, band)] = low(
-        jnp.concatenate([wide(slab_in[j]) for j in range(seq_count)], axis=0)
-    )
-    self_view = lambda index: cols.at[block(index, band), lanes(384, 768)]
-    cross_view = lambda index: cols.at[block(index, band), lanes(0, 384)]
-    up_view = lambda index: cols.at[block(index, band), lanes(1152, hidden)]
-    down_view = lambda index: down_all.at[block(index, band)]
-    out_view = lambda index: out_all.at[index]
+    cols, halves = m.cols, m.halves
+    rows = jnp.concatenate([wide(slab_in[j]) for j in range(seq_count)], axis=0)
+    cols[block(d, band), 0:768] = low(rows[:, 0:768])
+    cols[block(d, band), 768 : 768 + hidden] = low(rows[:, 1536 : 1536 + hidden])
+    rows = rows[:, 768:1536]
+    rows = jnp.where(core == 0, rows[0 : band // 2], rows[band // 2 : band])
+    halves[d, core] = low(rows)
+
+    def group_view(full, half, first):
+        place = lanes(first, 384)
+        return lambda index: [
+            full.at[block(index, band), place],
+            half.at[index, core, :, place],
+        ]
+
+    def half_cols(first, size):
+        return halves[:, :, :, first : first + size].reshape(width, size)
+
+    def half_swap(first):
+        part = halves.at[:, core, :, lanes(first, 384)]
+        return begin(part, part, (d, sibling))
+
+    self_view, cross_view = group_view(cols, halves, 384), group_view(cols, halves, 0)
+    up_view = lambda index: [cols.at[block(index, band), lanes(768, hidden)]]
+    down_view = lambda index: [down_all.at[block(index, band)]]
     self_ag = gather_far(self_view)
     gather_near(self_ag)
-    out_ag = gather_far(out_view)
-    gather_near(out_ag)
-
-    arrive(vec_dp)
+    gather_step(out_ag, 0)
+    gather_step(out_ag, 1)
+
+    arrive(vec_seq)
     stacked = vec_all[...].reshape(data_count * seq_count * 16, LANES)
     row_of = lax.broadcasted_iota(jnp.int32, (LANES, width), 0)
     col_of = lax.broadcasted_iota(jnp.int32, (LANES, width), 1)
@@ -979,55 +1034,60 @@
     h1, h2, h3, e1, e2 = m.h1, m.h2, m.h3, m.e1, m.e2
     h1[block(s, tokens)] = low(text_unit * vector(1) + vector(2))
     h1_ag = seq_gather(rows_of(h1))
-    cot_ag = seq_gather(rows_of(cot_all))
-
-    outbox, tiles = m.outbox, m.tiles
-    rest_rows, rest_wide, rest_out, rest_in = m.rest_rows, m.rest_wide, m.rest_out, m.rest_in
-    normed = [wide(low(unit * vector(5) + vector(6))) for unit in tile_units]
-    for p in range(data_count):
-        total = normed[0] * route[p][0]
-        for t in range(1, tile_count):
-            total = total + normed[t] * route[p][t]
-        outbox[block(p, main)] = low(total[0:main])
-        rest_rows[p : p + 1] = total[main:real_rows]
-    for k in range(columns):
-        rest_wide[pl.ds(k, data_count, stride=16), :] = rest_rows[:, LANES * k : LANES * (k + 1)]
-    rest_out[...] = low(rest_wide[0 : 16 * data_count]).reshape(rest_out.shape)
-    own_slot = block(s * data_count + d, main)
-    tiles[own_slot] = outbox[block(d, main)]
-    rest_in[s, d] = rest_out[d]
-
-    tile_dp = []
-
-    def tile_out(k):
-        peer = (d + k) % data_count
-        tile_dp.append(begin(outbox.at[block(peer, main)], tiles.at[own_slot], (peer, s)))
-        tile_dp.append(begin(rest_out.at[peer], rest_in.at[s, d], (peer, s)))
-
-    for k in range(2, data_count, 2):
-        tile_out(k)
+
+    arrive(tile_dp)
+    whole_place = block(s, inbox)
+    tiles[whole_place] = low(wide(tiles[whole_place]) * vector(5) + vector(6))
+    whole_own = tiles.at[block(s, inbox)]
+    tile_pair = [
+        begin(whole_own, whole_own, (d, sibling)),
+        begin(rest_in.at[s], rest_in.at[s], (d, sibling)),
+    ]
+    rest_far = begin(rest_in.at[s], rest_in.at[s], (d, across))
+    quarter = inbox // 4
+
+    def quarter_of(index, k):
+        return tiles.at[pl.ds(pl.multiple_of(index * inbox + k * quarter, quarter), quarter)]
+
+    def tile_send(k):
+        part = quarter_of(s, k)
+        return begin(part, part, (d, across))
+
+    def tile_pass(k):
+        tile_far[k].wait_recv()
+        part = quarter_of(across, k)
+        tile_pair.append(begin(part, part, (d, sibling)))
+
+    tile_far = [tile_send(k) for k in range(4)]
+    gather_step(out_ag, 2)
+    gather_step(self_ag, 0)
+    gather_step(self_ag, 1)
     seq_pass(h1_ag)
-    gather_forward(self_ag)
-    seq_pass(cot_ag)
-    gather_forward(out_ag)
-    for k in range(1, data_count, 2):
-        tile_out(k)
+    gather_end(out_ag)
+    per_seq = data_count // seq_count
+    out_in = m.out_in
+    out_seq = []
+    for peer in (across, corner, sibling):
+        out_seq.append(
+            begin(out_all.at[pl.ds(peer * per_seq, per_seq)], out_in.at[s], (d, peer))
+        )
+    out_in[s] = out_all[pl.ds(s * per_seq, per_seq)]
     cross_ag = gather_far(cross_view)
+    gather_near(cross_ag)
+    gather_step(self_ag, 2)
     up_ag = gather_far(up_view)
     down_ag = gather_far(down_view)
-    gather_near(cross_ag)
-    gather_near(up_ag)
-    gather_near(down_ag)
     gather_end(self_ag)
-    halves = m.halves
-    half_place = pl.ds(pl.multiple_of(core * 384, 384), 384)
-    half_copy = begin(cols.at[:, lanes(768, 384)], halves.at[:, half_place], (d, sibling))
-    halves[:, half_place] = cols[:, 768:1152]
+    half_copy = half_swap(384)
     seq_end(h1_ag)
     qkv1, qm1, p1, o1 = m.qkv1, m.qm1, m.p1, m.o1
     qkv1[:, 0:384] = low(dot_plain(h1[...], cols[:, 384:768]))
     arrive([half_copy])
-    qkv1[:, 384:768] = low(dot_plain(h1[...], halves[:, 384:768]))
+    qkv1[:, 384:768] = low(dot_plain(h1[...], half_cols(384, 384)))
+    gather_step(cross_ag, 0)
+    gather_step(cross_ag, 1)
+    gather_near(up_ag)
+    gather_near(down_ag)
 
     spot_q = lax.broadcasted_iota(jnp.int32, (length, length), 0)
     spot_k = lax.broadcasted_iota(jnp.int32, (length, length), 1)
@@ -1048,15 +1108,28 @@
     o1[:, 0:128] = low(mixed[0] + mixed[1])
     o1[:, 128:256] = low(mixed[2])
 
-    gather_end(out_ag)
-    per_seq = data_count // seq_count
-    out_in = m.out_in
-    out_seq = []
-    for peer in seq_peers:
-        out_seq.append(
-            begin(out_all.at[pl.ds(peer * per_seq, per_seq)], out_in.at[s], (d, peer))
-        )
-    out_in[s] = out_all[pl.ds(s * per_seq, per_seq)]
+    arrive(out_seq)
+    out_rows = m.out_rows
+    natural = jnp.concatenate(
+        [wide(out_in[j, i]) for i in range(per_seq) for j in range(seq_count)], axis=0
+    )
+    blank = jnp.zeros((64, 2 * width), jnp.float32)
+    even = jnp.concatenate([natural, blank], axis=0)
+    odd = jnp.concatenate([natural[64:192], blank, natural[0:64]], axis=0)
+    out_rows[...] = low(jnp.where(core == 0, even, odd))
+
+    state = seq_sum_begin(0, lambda i, j: dot_plain(pick(o1, i, j), out_rows[:, 0:width]))
+    state = seq_sum_pass(state)
+    gather_step(cross_ag, 2)
+    x2, x3, dx = m.x2, m.x3, m.dx
+    second = wide(text[0]) + seq_sum_end(state)
+    x2[...] = second
+    unit, _ = norm_parts(second)
+    h2[block(s, tokens)] = low(unit * vector(3) + vector(4))
+    h2_ag = seq_gather(rows_of(h2))
+    cot_ag = seq_gather(rows_of(cot_all))
+    gather_step(up_ag, 0)
+    gather_step(up_ag, 1)
     row_up = lax.broadcasted_iota(jnp.int32, (LANES, hidden), 0)
     col_up = lax.broadcasted_iota(jnp.int32, (LANES, hidden), 1)
     spread = dot_plain(stacked, jnp.where(row_up == col_up % band, 1.0, 0.0).astype(jnp.bfloat16))
@@ -1066,58 +1139,17 @@
     picked = jnp.where(which == (column // band) * seq_count + s, spread, 0.0)
     m.up_bias[...] = jnp.sum(picked, axis=0)[9:10]
 
-    arrive(tile_dp)
-    whole_own = tiles.at[block(s, inbox)]
-    tile_pair = [
-        begin(whole_own, whole_own, (d, sibling)),
-        begin(rest_in.at[s], rest_in.at[s], (d, sibling)),
-    ]
-    rest_far = begin(rest_in.at[s], rest_in.at[s], (d, across))
-    quarter = inbox // 4
-
-    def quarter_of(index, k):
-        return tiles.at[pl.ds(pl.multiple_of(index * inbox + k * quarter, quarter), quarter)]
-
-    def tile_send(k):
-        part = quarter_of(s, k)
-        return begin(part, part, (d, across))
-
-    def tile_pass(k):
-        tile_far[k].wait_recv()
-        part = quarter_of(across, k)
-        tile_pair.append(begin(part, part, (d, sibling)))
-
-    tile_far = [tile_send(0)]
-    arrive(out_seq)
-    out_rows = m.out_rows
-    natural = jnp.concatenate(
-        [wide(out_in[j, i]) for i in range(per_seq) for j in range(seq_count)], axis=0
-    )
-    blank = jnp.zeros((64, 2 * width), jnp.float32)
-    even = jnp.concatenate([natural, blank], axis=0)
-    odd = jnp.concatenate([natural[64:192], blank, natural[0:64]], axis=0)
-    out_rows[...] = low(jnp.where(core == 0, even, odd))
-
-    state = seq_sum_begin(0, lambda i, j: dot_plain(pick(o1, i, j), out_rows[:, 0:width]))
-    state = seq_sum_pass(state)
-    tile_far.append(tile_send(1))
-    x2, x3, dx = m.x2, m.x3, m.dx
-    second = wide(text[0]) + seq_sum_end(state)
-    x2[...] = second
-    unit, _ = norm_parts(second)
-    h2[block(s, tokens)] = low(unit * vector(3) + vector(4))
-    h2_ag = seq_gather(rows_of(h2))
-    tile_far += [tile_send(2), tile_send(3)]
 
     kv2, qm2, pr, o2, o_acc = m.kv2, m.qm2, m.pr, m.o2, m.o_acc
 
     def keys_values(here):
         rows = tiles[here]
         kv2[here, 0:256] = low(dot_plain(rows, cols[:, 128:384]))
-        kv2[here, 256:512] = low(dot_plain(rows, halves[:, 128:384]))
-
-    gather_forward(cross_ag)
+        kv2[here, 256:512] = low(dot_plain(rows, half_cols(128, 256)))
+
     gather_end(cross_ag)
+    half_copy = half_swap(0)
+    arrive([half_copy])
     keys_values(block(s, inbox))
     tile_pass(0)
     seq_pass(h2_ag)
@@ -1126,13 +1158,14 @@
     tile_pass(1)
     rest_far.wait_recv()
     tile_pair.append(begin(rest_in.at[across], rest_in.at[across], (d, sibling)))
-    gather_step(up_ag, 0)
+    gather_step(up_ag, 2)
+    gather_step(down_ag, 0)
     seq_end(h2_ag)
     query_full = dot_plain(h2[...], cols[:, 0:128])
-    query_half = dot_plain(h2[...], halves[:, 0:128])
+    query_half = dot_plain(h2[...], half_cols(0, 128))
     for head in range(3):
         source = query_full if head < 2 else query_half
-        qm2[block(head, length)] = low(wide(low(source)) * head_masks[head])
+        qm2[block(head, length)] = low(wide(low(source)) * (head_masks[head] * factor))
     tile_pass(2)
     tile_pass(3)
     keys_values(block(across, inbox))
@@ -1140,30 +1173,27 @@
     keys_values(block(corner, inbox))
     rest_wide[...] = wide(rest_in[...]).reshape(rest_wide.shape)
     for k in range(columns):
-        tiles[keys_main:keys, LANES * k : LANES * (k + 1)] = low(
-            rest_wide[pl.ds(k, rests, stride=16), :]
+        place = slice(LANES * k, LANES * (k + 1))
+        tiles[keys_main:keys, place] = low(
+            rest_wide[pl.ds(k, rests, stride=16), :] * vec[5:6, place] + vec[6:7, place]
         )
     keys_values(pl.ds(keys_main, rests))
-    gather_step(up_ag, 1)
-    gather_step(up_ag, 2)
+    gather_step(down_ag, 1)
     for head in range(3):
         base = 256 * (head // 2)
         place = 128 * (head // 2)
 
-        @pl.loop(0, seq_count)
-        def _(i):
-            here = block(head * seq_count + i, tokens)
-            scores = dot_right(qm2[here], kv2[:, base : base + 128]) * factor + m.key_bias[...]
-            exponent = jnp.exp(scores - jnp.max(scores, axis=1, keepdims=True))
-            chances = low(exponent / jnp.sum(exponent, axis=1, keepdims=True))
-            pr[here] = chances
-            result = dot_plain(chances, kv2[:, base + 128 : base + 256]) * head_masks[head]
-            if head == 1:
-                result = result + o_acc[block(i, tokens), place : place + 128]
-            o_acc[block(i, tokens), place : place + 128] = result
-
-        if head < 2:
-            gather_step(down_ag, head)
+        here = block(head, length)
+        scores = dot_right(qm2[here], kv2[:, base : base + 128]) + m.key_bias[...]
+        exponent = jnp.exp(scores - jnp.max(scores, axis=1, keepdims=True))
+        chances = low(exponent * (1.0 / jnp.sum(exponent, axis=1, keepdims=True)))
+        pr[here] = chances
+        result = dot_plain(chances, kv2[:, base + 128 : base + 256]) * head_masks[head]
+        if head == 1:
+            result = result + o_acc[:, place : place + 128]
+        o_acc[:, place : place + 128] = result
+        if head == 0:
+            gather_step(down_ag, 2)
 
     o2[...] = low(o_acc[...])
     state = seq_sum_begin(
@@ -1175,9 +1205,9 @@
     unit, _ = norm_parts(third)
     h3[block(s, tokens)] = low(unit * vector(7) + vector(8))
     h3_ag = seq_gather(rows_of(h3))
+    seq_pass(cot_ag)
     seq_end(cot_ag)
     seq_pass(h3_ag)
-    gather_step(down_ag, 2)
     gather_end(down_ag)
     act, slope, du = m.act, m.slope, m.du
     slope[...] = dot_right(cot_all[...], down_all[...])
@@ -1187,7 +1217,7 @@
     @pl.loop(0, seq_count)
     def _(i):
         here = block(i, tokens)
-        pre = dot_plain(h3[here], cols[:, 1152 : 1152 + hidden]) + m.up_bias[...]
+        pre = dot_plain(h3[here], cols[:, 768 : 768 + hidden]) + m.up_bias[...]
         cdf = 0.5 * (1.0 + lax.erf(pre * (1.0 / math.sqrt(2.0))))
         density = jnp.exp(-0.5 * pre * pre) * (1.0 / math.sqrt(2.0 * math.pi))
         act[here] = low(pre * cdf)
@@ -1195,13 +1225,13 @@
         du[here] = low(grad * (cdf + pre * density))
 
     state = seq_sum_begin(
-        2, lambda i, j: dot_right(pick(du, i, j), cols[:, 1152 : 1152 + hidden])
+        2, lambda i, j: dot_right(pick(du, i, j), cols[:, 768 : 768 + hidden])
     )
     state = seq_sum_pass(state)
     g_cols, g_down = m.g_cols, m.g_down
     g_down[...] = low(dot_left(act[...], cot_all[...]))
-    g_down_view = lambda index: g_down.at[block(index, band)]
-    down_rs = sum_begin(g_down_view, m.y_down, m.z_down)
+    g_down_view = lambda index: [g_down.at[block(index, band)]]
+    down_rs = sum_begin(g_down_view, [m.y_down], [m.z_down])
     grad_mid = seq_sum_end(state)
     unit, inverse = norm_parts(x3[...])
     vv = m.vv
@@ -1216,9 +1246,9 @@
     vv[8:9] = column_sum(grad_mid)
     vv[9:10, 0:hidden] = column_sum(wide(du[...]))
 
-    g_cols[:, 1152 : 1152 + hidden] = low(dot_left(h3[...], du[...]))
-    g_up_view = lambda index: g_cols.at[block(index, band), lanes(1152, hidden)]
-    up_rs = sum_begin(g_up_view, m.y_up, m.z_up)
+    g_cols[:, 768 : 768 + hidden] = low(dot_left(h3[...], du[...]))
+    g_up_view = lambda index: [g_cols.at[block(index, band), lanes(768, hidden)]]
+    up_rs = sum_begin(g_up_view, [m.y_up], [m.z_up])
     sum_step(down_rs, 0)
     seq_pass(e2_ag)
     sum_step(down_rs, 1)
@@ -1234,29 +1264,26 @@
         base = 256 * (head // 2)
         place = 128 * (head // 2)
 
-        @pl.loop(0, seq_count)
-        def _(i):
-            here = block(head * seq_count + i, tokens)
-            chances = wide(pr[here])
-            grad_p = dot_right(dom[here], kv2[:, base + 128 : base + 256])
-            weighted = jnp.sum(chances * grad_p, axis=1, keepdims=True)
-            grad_s = low(chances * (grad_p - weighted))
-            ds[here] = grad_s
-            result = dot_plain(grad_s, kv2[:, base : base + 128]) * (head_masks[head] * factor)
-            if head == 1:
-                result = result + o_acc[block(i, tokens), place : place + 128]
-            o_acc[block(i, tokens), place : place + 128] = result
-
+        here = block(head, length)
+        chances = wide(pr[here])
+        grad_p = dot_right(dom[here], kv2[:, base + 128 : base + 256])
+        weighted = jnp.sum(chances * grad_p, axis=1, keepdims=True)
+        grad_s = low(chances * (grad_p - weighted))
+        ds[here] = grad_s
+        result = dot_plain(grad_s, kv2[:, base : base + 128]) * (head_masks[head] * factor)
+        if head == 1:
+            result = result + o_acc[:, place : place + 128]
+        o_acc[:, place : place + 128] = result
         if head < 2:
             sum_step(down_rs, 2 + head)
 
     dq2[...] = low(o_acc[...])
+    sum_step(up_rs, 0)
     state = seq_sum_begin(
         4,
         lambda i, j: dot_right(pick(dq2, i, j, slice(0, 128)), cols[:, 0:128])
-        + dot_right(pick(dq2, i, j, slice(128, 256)), halves[:, 0:128]),
-    )
-    state = seq_sum_pass(state)
+        + dot_right(pick(dq2, i, j, slice(128, 256)), half_cols(0, 128)),
+    )
 
     g_out, g_out_send = m.g_out, m.g_out_send
 
@@ -1275,7 +1302,19 @@
         return copies
 
     xout_seq = out_grad(1, dot_left(o2[...], e2[...]))
-    sum_step(up_rs, 0)
+    state = seq_sum_pass(state)
+    for tile in range(2):
+        first, count = (0, 2 * length) if tile == 0 else (2 * length, length)
+        base = 256 * tile
+        for start, size in spans(0, keys, 512):
+            cut = slice(start, start + size)
+            dkv2[cut, base : base + 128] = low(
+                dot_left(ds[first : first + count, cut], qm2[first : first + count])
+            )
+            dkv2[cut, base + 128 : base + 256] = low(
+                dot_left(pr[first : first + count, cut], dom[first : first + count])
+            )
+    sum_step(up_rs, 1)
     second_grad = seq_sum_end(state)
     unit, inverse = norm_parts(x2[...])
     dx2 = dx[...] + norm_back(unit, inverse, vector(3), second_grad)
@@ -1284,30 +1323,17 @@
     e1_ag = seq_gather(rows_of(e1))
     vv[3:4] = column_sum(second_grad * unit)
     vv[4:5] = column_sum(second_grad)
-    sum_step(up_rs, 1)
+    sum_step(up_rs, 2)
     arrive(xout_seq)
-    xout_view = lambda index: g_out.at[index, :, lanes(width, width)]
-    xout_rs = sum_begin(xout_view, m.y_xout, m.z_xout)
-
-    for tile in range(2):
-        first, count = (0, 2 * length) if tile == 0 else (2 * length, length)
-        base = 256 * tile
-        for start, size in spans(0, keys, 512):
-            cut = slice(start, start + size)
-            dkv2[cut, base : base + 128] = low(
-                dot_left(ds[first : first + count, cut], qm2[first : first + count]) * factor
-            )
-            dkv2[cut, base + 128 : base + 256] = low(
-                dot_left(pr[first : first + count, cut], dom[first : first + count])
-            )
-    seq_pass(e1_ag)
-    sum_step(up_rs, 2)
+    xout_view = lambda index: [g_out.at[index, :, lanes(width, width)]]
+    xout_rs = sum_begin(xout_view, [m.y_xout], [m.z_xout])
+
     dn = m.dn
 
     def tile_grads(here):
         dn[here] = low(
             dot_right(dkv2[here, 0:256], cols[:, 128:384])
-            + dot_right(dkv2[here, 256:512], halves[:, 128:384])
+            + dot_right(dkv2[here, 256:512], half_cols(128, 256))
         )
 
     dr_out, dr_pair, dr_far, dr_home = m.dr_out, m.dr_pair, m.dr_far, m.dr_home
@@ -1326,6 +1352,7 @@
         for k, peer in enumerate((sibling, corner))
     ]
     tile_grads(block(across, inbox))
+    seq_pass(e1_ag)
     pair_far.wait_recv()
     fold = dn.at[block(across, inbox)]
     fold[...] = low(wide(fold[...]) + wide(dn_pair[1]))
@@ -1339,30 +1366,21 @@
     def quarter_in(ref, index, k):
         return ref.at[pl.ds(pl.multiple_of(index * inbox + k * quarter, quarter), quarter)]
 
-    far_copies = [far_send(0)]
-    g_half, g_half2, half_in = m.g_half, m.g_half2, m.half_in
-    grad = dot_left(h2[...], dq2[...])
-    g_cols[:, 0:128] = low(grad[:, 0:128])
-    g_half[:, 0:128] = low(grad[:, 128:256])
-    for cut in range(3):
-        span = slice(256 * cut, 256 * cut + 256)
-        grad = dot_left(tiles[:, span], dkv2[...])
-        g_cols[span, 128:384] = low(grad[:, 0:256])
-        g_half[span, 128:384] = low(grad[:, 256:512])
-    half_cross = links.make(g_half, half_in, (d, sibling))
-
-    @pl.when(core == 1)
-    def _():
-        half_cross.start()
-
-    g_cross_view = lambda index: g_cols.at[block(index, band), lanes(0, 384)]
-    cross_rs = sum_begin(g_cross_view, m.y_cross, m.z_cross)
-    far_copies += [far_send(1)]
-    tile_grads(block(sibling, inbox))
-    pair_own = begin(dn.at[block(sibling, inbox)], dn_pair.at[0], (d, sibling))
-    tile_grads(block(s, inbox))
+    far_copies = [far_send(k) for k in range(4)]
     sum_step(up_rs, 3)
-    sum_middle(xout_rs)
+    g_half, half_in, g_cross = m.g_half, m.half_in, m.g_cross
+    half_shape = (data_count, 2, band // 2)
+
+    def half_send(first):
+        place = lanes(first, 384)
+        return begin(g_half.at[:, 1 - core, :, place], half_in.at[:, :, place], (d, sibling))
+
+    def half_add(first, copy):
+        copy.wait_recv()
+        place = lanes(first, 384)
+        g_half[:, core, :, place] = low(
+            wide(g_half[:, core, :, place]) + wide(half_in[:, :, place])
+        )
 
     seq_end(e1_ag)
     grad_o = low(dot_right(e1[...], out_rows[:, 0:width]))
@@ -1390,74 +1408,88 @@
     state = seq_sum_begin(
         5,
         lambda i, j: dot_right(pick(dqkv, i, j, slice(0, 384)), cols[:, 384:768])
-        + dot_right(pick(dqkv, i, j, slice(384, 768)), halves[:, 384:768]),
+        + dot_right(pick(dqkv, i, j, slice(384, 768)), half_cols(384, 384)),
     )
 
     grad = dot_left(h1[...], dqkv[...])
     g_cols[:, 384:768] = low(grad[:, 0:384])
-    g_half2[...] = low(grad[:, 384:768])
-    half_self = links.make(g_half2, half_in, (d, sibling))
-
-    @pl.when(core == 0)
-    def _():
-        half_self.start()
-
+    g_half[:, :, :, 384:768] = low(grad[:, 384:768]).reshape(*half_shape, 384)
+    half_copy = half_send(384)
     state = seq_sum_pass(state)
     sout_seq = out_grad(0, dot_left(o1[...], e1[...]))
-    far_copies += [far_send(2), far_send(3)]
-    g_self_view = lambda index: g_cols.at[block(index, band), lanes(384, 768)]
-
-    @pl.when(core == 0)
-    def _():
-        half_cross.wait_recv()
-        g_cols[:, 768:1152] = low(wide(g_half[...]) + wide(half_in[...]))
-
-    @pl.when(core == 1)
-    def _():
-        half_self.wait_recv()
-        g_cols[:, 768:1152] = low(wide(g_half2[...]) + wide(half_in[...]))
-
-    self_rs = sum_begin(g_self_view, m.y_self, m.z_self)
+    half_add(384, half_copy)
+    self_rs = sum_begin(
+        group_view(g_cols, g_half, 384),
+        [m.y_full.at[:, :, lanes(384, 384)], m.y_half.at[:, :, lanes(384, 384)]],
+        [m.z_full.at[:, :, lanes(384, 384)], m.z_half.at[:, :, lanes(384, 384)]],
+    )
+    out_state = seq_sum_begin(3, lambda i, j: dot_plain(pick(act, i, j), down_all[...]))
+    tile_grads(block(sibling, inbox))
+    pair_own = begin(dn.at[block(sibling, inbox)], dn_pair.at[0], (d, sibling))
+    tile_grads(block(s, inbox))
+
+    sum_middle(xout_rs)
+    out_state = seq_sum_pass(out_state)
+    grad = dot_left(h2[...], dq2[...])
+    g_cols[:, 0:128] = low(grad[:, 0:128])
+    g_half[:, :, :, 0:128] = low(grad[:, 128:256]).reshape(*half_shape, 128)
+    for cut in range(3):
+        span = slice(256 * cut, 256 * cut + 256)
+        grad = dot_left(tiles[:, span], dkv2[...])
+        g_cols[span, 128:384] = low(grad[:, 0:256])
+        g_cross[span] = low(grad[:, 256:512])
+    g_half[:, :, :, 128:384] = g_cross[...].reshape(*half_shape, 256)
+    half_copy = half_send(0)
+    sum_step(self_rs, 0)
+    half_add(0, half_copy)
+    cross_rs = sum_begin(
+        group_view(g_cols, g_half, 0),
+        [m.y_full.at[:, :, lanes(0, 384)], m.y_half.at[:, :, lanes(0, 384)]],
+        [m.z_full.at[:, :, lanes(0, 384)], m.z_half.at[:, :, lanes(0, 384)]],
+    )
+    sum_step(self_rs, 1)
     arrive(sout_seq)
-    sout_view = lambda index: g_out.at[index, :, lanes(0, width)]
-    sout_rs = sum_begin(sout_view, m.y_sout, m.z_sout)
-    sum_middle(cross_rs)
-
+    sout_view = lambda index: [g_out.at[index, :, lanes(0, width)]]
+    sout_rs = sum_begin(sout_view, [m.y_sout], [m.z_sout])
+    sum_step(self_rs, 2)
+    sum_step(self_rs, 3)
+    sum_step(cross_rs, 0)
+    sum_step(cross_rs, 1)
+    first_grad = seq_sum_end(state)
+    unit, inverse = norm_parts(wide(text[0]))
+    vv[1:2] = column_sum(first_grad * unit)
+    vv[2:3] = column_sum(first_grad)
+    r_tgrad[...] = low(dx[...] + norm_back(unit, inverse, vector(1), first_grad))
     arrive([pair_own, rest_far])
     dr_out[s] = low(wide(dr_out[s]) + wide(dr_pair[0]) + wide(dr_far[...]))
+
+    home_dp = []
+    own_home = block(d, main)
     for k in range(4):
         far_copies[k].wait_recv()
         mine = quarter_in(dn, s, k)
         there = block(k, quarter)
         mine[...] = low(wide(mine[...]) + wide(dn_pair[0, there]) + wide(dn_far[there]))
-    home_dp = []
-    own_home = block(d, main)
-    for k in range(1, data_count):
+
+    def home_send(k):
         peer = (d + k) % data_count
         source = dn.at[block(s * data_count + peer, main)]
         home_dp.append(begin(source, dn_home.at[own_home], (peer, s)))
         home_dp.append(begin(dr_out.at[s, peer], dr_home.at[d], (peer, s)))
+
+    for k in (2, 1, 4, 3, 6, 5, 7):
+        home_send(k)
     dn_home[own_home] = dn[block(s * data_count + d, main)]
     dr_home[d] = dr_out[s, d]
-
-    first_grad = seq_sum_end(state)
-    unit, inverse = norm_parts(wide(text[0]))
-    vv[1:2] = column_sum(first_grad * unit)
-    vv[2:3] = column_sum(first_grad)
-    r_tgrad[...] = low(dx[...] + norm_back(unit, inverse, vector(1), first_grad))
-    out_state = seq_sum_begin(3, lambda i, j: dot_plain(pick(act, i, j), down_all[...]))
-    out_state = seq_sum_pass(out_state)
-
-    sum_middle(self_rs)
+    sum_step(cross_rs, 2)
+    sum_step(cross_rs, 3)
     sum_middle(sout_rs)
     r_text[...] = low(x3[...] + seq_sum_end(out_state) + vector(0))
 
-    cols_out, cols_in = m.cols_out, m.cols_in
-
-    def finish_cols(first, size, state):
-        total = low(sum_end(state))
+    cols_out, cols_in, ends_out, ends_in = m.cols_out, m.cols_in, m.ends_out, m.ends_in
+
+    def finish_cols(first, size, total):
         place = lanes(first, size)
-        total = wide(total)
         for j in range(seq_count):
             cols_out[j, :, place] = low(total[shard * j : shard * (j + 1)])
         cols_in[s, :, place] = cols_out[s, :, place]
@@ -1466,10 +1498,21 @@
             for peer in seq_peers
         ]
 
-    r_down[...] = sum_end(down_rs)
-    ends = finish_cols(1152, hidden, up_rs)
-    r_outs[1] = sum_end(xout_rs)
-    ends += finish_cols(0, 384, cross_rs)
+    def finish_half(first, total):
+        place = lanes(first, 384)
+        for j in range(2):
+            ends_out[j, :, place] = low(total[shard * j : shard * (j + 1)])
+        ends_in[s, :, place] = ends_out[core, :, place]
+        return [
+            begin(ends_out.at[peer % 2, :, place], ends_in.at[s, :, place], (d, peer))
+            for peer in seq_peers
+        ]
+
+    (r_down[...],) = sum_end(down_rs)
+    ends = finish_cols(768, hidden, sum_end(up_rs)[0])
+    (r_outs[1],) = sum_end(xout_rs)
+    full, half = sum_end(self_rs)
+    ends += finish_cols(384, 384, full) + finish_half(384, half)
 
     arrive(home_dp)
     gain_sum = jnp.zeros((1, width), jnp.float32)
@@ -1503,8 +1546,9 @@
         vv_dp.append(begin(vv_out.at[peer], vv_in.at[d], (peer, s)))
     vv_in[d] = vv_out[d]
 
-    ends += finish_cols(384, 768, self_rs)
-    r_outs[0] = sum_end(sout_rs)
+    full, half = sum_end(cross_rs)
+    ends += finish_cols(0, 384, full) + finish_half(0, half)
+    (r_outs[0],) = sum_end(sout_rs)
 
     arrive(vv_dp)
     total = vv_in[0]
@@ -1516,6 +1560,7 @@
 
     arrive(ends)
     r_cols[...] = cols_in[...]
+    r_half[...] = ends_in[...]
     arrive(vq_seq)
     total = vq[0] + vq[1] + vq[2] + vq[3]
     r_vec[...] = pltpu.roll(total, (LANES - shard * s) % LANES, 1)
@@ -1524,38 +1569,29 @@
     for copy in links.started:
         copy.wait_send()
 
-    @pl.when(core == 0)
-    def _():
-        half_self.wait_send()
-
-    @pl.when(core == 1)
-    def _():
-        half_cross.wait_send()
-
-
-def unpack_kernel(t_out, t_grad, i_grad, cols, outs, down, vec, *results):
+
+def unpack_kernel(t_out, t_grad, i_grad, cols, ends, outs, down, vec, *results):
     o_text, o_tgrad, o_igrad, o_q, o_k, o_v, o_o, o_xq, o_xk, o_xv, o_xo, o_up, o_down, *vectors = (
         results
     )
     seq_count, shard, total = cols.shape
-    hidden = total - 1152
+    hidden = total - 768
+    core = lax.axis_index("seq") // 2
     band = down.shape[0]
     o_text[0] = t_out[...]
     o_tgrad[0] = t_grad[...]
     o_igrad[...] = i_grad[...]
     for k, result in enumerate((o_xq, o_xk, o_xv, o_q, o_k, o_v)):
         here = slice(LANES * k, LANES * (k + 1))
-        there = slice(768 + LANES * (k % 3), 768 + LANES * (k % 3 + 1))
-        carrier = k // 3
         for j, tile in ((0, 0), (1, 2), (2, 3), (3, 5)):
             result[:, LANES * tile : LANES * (tile + 1)] = wide(cols[j, :, here])
-        for j, tile in ((carrier, 1), (2 + carrier, 4)):
-            result[:, LANES * tile : LANES * (tile + 1)] = wide(cols[j, :, there])
+        for j, tile in ((0, 1), (2, 4)):
+            result[:, LANES * tile : LANES * (tile + 1)] = wide(ends[j + core, :, here])
     o_o[...] = outs[0]
     o_xo[...] = outs[1]
     o_down[...] = down[...]
     lane = lax.broadcasted_iota(jnp.int32, (1, LANES), 1)
-    parts = [wide(cols[j, :, 1152:total]) for j in range(seq_count)]
+    parts = [wide(cols[j, :, 768:total]) for j in range(seq_count)]
     for tile in range(hidden * seq_count // LANES):
         pieces = []
         for at, size in spans(LANES * tile, LANES * tile + LANES, band):
@@ -1596,7 +1632,8 @@
         row_out,
         row_out,
         jax.ShapeDtypeStruct(image_in.shape, jnp.bfloat16),
-        jax.ShapeDtypeStruct((seq_count, shard, 1152 + hidden), jnp.bfloat16),
+        jax.ShapeDtypeStruct((seq_count, shard, 768 + hidden), jnp.bfloat16),
+        jax.ShapeDtypeStruct((seq_count, shard, 768), jnp.bfloat16),
         jax.ShapeDtypeStruct((2, shard, width), jnp.float32),
         jax.ShapeDtypeStruct((band, width), jnp.float32),
         jax.ShapeDtypeStruct((16, LANES), jnp.float32),

time: 199 us -> 178 us (0.89)
  Pallas kernels: 195 us -> 174 us
    pallas_call x1, Pallas kernels: 192 us -> 171 us  [fused_device(): pl.pallas_call(partial(fused_kernel, names, len(inputs)), out_shape=packe...]
where the time goes in v2:
time: 178 us
  Pallas kernels  174 us (98%)
  local copies, waits for them, and re-layouts  3.53 us (2%)
    pallas_call x1, Pallas kernels, fused_device(): pl.pallas_call(partial(fused_kernel, names, len(inputs)), out_shape=packe...  171 us

profile of v2, /device:TPU:0, one launch (start us, length us, event | category | flops | bytes accessed | tf_op | source)
XLA Modules:
  0.0 178.0 jit_solution(15031456137363261905)
XLA Ops:
  0.7 1.7 copy.48.refs_3_
  2.4 171.1 %decoder_layer.1 = (bf16[64,768]{1,0:T(8,128)(2,1)}, bf16[64,768]{1,0:T(8,128)(2,1)}, bf16[4,49,768]{2,1,0:T(8,128)(2,1)}, bf16[4,24,1536]{2,1,0:T(8,128)(2,1)},...) custom-call(s32[32]{0:T(128)} %refs_0_.1, s32[8]{0:T(128)} %refs_1_.1, ...), custom_call_target="tpu_custom_call" | custom-call | tf_op jit(solution)/shard_map/decoder_layer/pallas_call | solution.py:1645
  173.5 2.7 %unpack.1 = (bf16[1,64,768]{2,1,0:T(8,128)(2,1)}, bf16[1,64,768]{2,1,0:T(8,128)(2,1)}, bf16[4,49,768]{2,1,0:T(8,128)(2,1)}, f32[24,768]{1,0:T(8,128)}, f32[24,76...) custom-call(bf16[64,768]{1,0:T(8,128)(2,1)} %get-tuple-element.31.t_, ...), custom_call_target="tpu_custom_call" | custom-call | tf_op jit(solution)/shard_map/unpack/pallas_call | solution.py:1668
  176.2 1.8 %copy.49 = bf16[4,49,768]{2,0,1:T(4,128)(2,1)} copy(bf16[4,49,768]{2,1,0:T(8,128)(2,1)} %get-tuple-element.41) | data formatting | bytes 602112 | tf_op jit(solution)/shard_map/unpack/pallas_call | solution.py:1668

commit v3 on v2

--- a/solution.py
+++ b/solution.py
@@ -642,6 +642,7 @@
         out_rows=((256, 2 * width), bf16),
         down_all=((hidden, width), bf16),
         outbox=((inbox, width), bf16),
+        units=((inbox, width), bf16),
         rest_rows=((data_count, width), f32),
         rest_wide=((rests * 16, LANES), f32),
         rest_out=((data_count, 16, LANES), bf16),
@@ -813,9 +814,12 @@
     def send_all(refs, device):
         return [begin(ref, ref, device) for ref in refs]
 
-    def gather_far(view):
-        own = view(d)
-        return view, [send_all(own, beyond), send_all(own, beside)], []
+    def gather_open(view):
+        return view, [], []
+
+    def gather_far(state):
+        own = state[0](d)
+        state[1].extend([send_all(own, beyond), send_all(own, beside)])
 
     def gather_near(state):
         state[2].extend(send_all(state[0](d), near))
@@ -930,6 +934,7 @@
     cot_all[block(s, tokens)] = cot[0]
     m.rest_wide[...] = jnp.zeros(m.rest_wide.shape, jnp.float32)
 
+
     def destination(index):
         total = jnp.int32(0)
         for k in range(slides):
@@ -981,7 +986,8 @@
     for k in (2, 1, 4, 3, 6, 5, 7):
         tile_out(k)
     out_view = lambda index: [out_all.at[index]]
-    out_ag = gather_far(out_view)
+    out_ag = gather_open(out_view)
+    gather_far(out_ag)
     gather_near(out_ag)
     arrive(vec_dp)
     vec_column = vec_all.at[:, s]
@@ -1012,11 +1018,11 @@
     self_view, cross_view = group_view(cols, halves, 384), group_view(cols, halves, 0)
     up_view = lambda index: [cols.at[block(index, band), lanes(768, hidden)]]
     down_view = lambda index: [down_all.at[block(index, band)]]
-    self_ag = gather_far(self_view)
-    gather_near(self_ag)
-    gather_step(out_ag, 0)
-    gather_step(out_ag, 1)
-
+    self_ag, cross_ag = gather_open(self_view), gather_open(cross_view)
+    up_ag, down_ag = gather_open(up_view), gather_open(down_view)
+    gather_far(self_ag)
+    for state in (self_ag, cross_ag, up_ag, down_ag):
+        gather_near(state)
     arrive(vec_seq)
     stacked = vec_all[...].reshape(data_count * seq_count * 16, LANES)
     row_of = lax.broadcasted_iota(jnp.int32, (LANES, width), 0)
@@ -1037,7 +1043,8 @@
 
     arrive(tile_dp)
     whole_place = block(s, inbox)
-    tiles[whole_place] = low(wide(tiles[whole_place]) * vector(5) + vector(6))
+    m.units[...] = tiles[whole_place]
+    tiles[whole_place] = low(wide(m.units[...]) * vector(5) + vector(6))
     whole_own = tiles.at[block(s, inbox)]
     tile_pair = [
         begin(whole_own, whole_own, (d, sibling)),
@@ -1059,9 +1066,13 @@
         tile_pair.append(begin(part, part, (d, sibling)))
 
     tile_far = [tile_send(k) for k in range(4)]
-    gather_step(out_ag, 2)
+    gather_step(out_ag, 0)
+    gather_step(out_ag, 1)
     gather_step(self_ag, 0)
     gather_step(self_ag, 1)
+    gather_step(out_ag, 2)
+    gather_far(cross_ag)
+    gather_far(up_ag)
     seq_pass(h1_ag)
     gather_end(out_ag)
     per_seq = data_count // seq_count
@@ -1072,11 +1083,7 @@
             begin(out_all.at[pl.ds(peer * per_seq, per_seq)], out_in.at[s], (d, peer))
         )
     out_in[s] = out_all[pl.ds(s * per_seq, per_seq)]
-    cross_ag = gather_far(cross_view)
-    gather_near(cross_ag)
     gather_step(self_ag, 2)
-    up_ag = gather_far(up_view)
-    down_ag = gather_far(down_view)
     gather_end(self_ag)
     half_copy = half_swap(384)
     seq_end(h1_ag)
@@ -1086,8 +1093,7 @@
     qkv1[:, 384:768] = low(dot_plain(h1[...], half_cols(384, 384)))
     gather_step(cross_ag, 0)
     gather_step(cross_ag, 1)
-    gather_near(up_ag)
-    gather_near(down_ag)
+    gather_far(down_ag)
 
     spot_q = lax.broadcasted_iota(jnp.int32, (length, length), 0)
     spot_k = lax.broadcasted_iota(jnp.int32, (length, length), 1)
@@ -1158,8 +1164,6 @@
     tile_pass(1)
     rest_far.wait_recv()
     tile_pair.append(begin(rest_in.at[across], rest_in.at[across], (d, sibling)))
-    gather_step(up_ag, 2)
-    gather_step(down_ag, 0)
     seq_end(h2_ag)
     query_full = dot_plain(h2[...], cols[:, 0:128])
     query_half = dot_plain(h2[...], half_cols(0, 128))
@@ -1168,6 +1172,8 @@
         qm2[block(head, length)] = low(wide(low(source)) * (head_masks[head] * factor))
     tile_pass(2)
     tile_pass(3)
+    gather_step(up_ag, 2)
+    gather_step(down_ag, 0)
     keys_values(block(across, inbox))
     arrive(tile_pair[2:])
     keys_values(block(corner, inbox))
@@ -1451,15 +1457,6 @@
     arrive(sout_seq)
     sout_view = lambda index: [g_out.at[index, :, lanes(0, width)]]
     sout_rs = sum_begin(sout_view, [m.y_sout], [m.z_sout])
-    sum_step(self_rs, 2)
-    sum_step(self_rs, 3)
-    sum_step(cross_rs, 0)
-    sum_step(cross_rs, 1)
-    first_grad = seq_sum_end(state)
-    unit, inverse = norm_parts(wide(text[0]))
-    vv[1:2] = column_sum(first_grad * unit)
-    vv[2:3] = column_sum(first_grad)
-    r_tgrad[...] = low(dx[...] + norm_back(unit, inverse, vector(1), first_grad))
     arrive([pair_own, rest_far])
     dr_out[s] = low(wide(dr_out[s]) + wide(dr_pair[0]) + wide(dr_far[...]))
 
@@ -1477,64 +1474,29 @@
         home_dp.append(begin(source, dn_home.at[own_home], (peer, s)))
         home_dp.append(begin(dr_out.at[s, peer], dr_home.at[d], (peer, s)))
 
-    for k in (2, 1, 4, 3, 6, 5, 7):
+    sum_step(self_rs, 2)
+    for k in (2, 4, 6):
+        home_send(k)
+    sum_step(self_rs, 3)
+    sum_step(cross_rs, 0)
+    sum_step(cross_rs, 1)
+    for k in (1, 3, 5, 7):
         home_send(k)
     dn_home[own_home] = dn[block(s * data_count + d, main)]
     dr_home[d] = dr_out[s, d]
-    sum_step(cross_rs, 2)
-    sum_step(cross_rs, 3)
-    sum_middle(sout_rs)
-    r_text[...] = low(x3[...] + seq_sum_end(out_state) + vector(0))
-
-    cols_out, cols_in, ends_out, ends_in = m.cols_out, m.cols_in, m.ends_out, m.ends_in
-
-    def finish_cols(first, size, total):
-        place = lanes(first, size)
-        for j in range(seq_count):
-            cols_out[j, :, place] = low(total[shard * j : shard * (j + 1)])
-        cols_in[s, :, place] = cols_out[s, :, place]
-        return [
-            begin(cols_out.at[peer, :, place], cols_in.at[s, :, place], (d, peer))
-            for peer in seq_peers
-        ]
-
-    def finish_half(first, total):
-        place = lanes(first, 384)
-        for j in range(2):
-            ends_out[j, :, place] = low(total[shard * j : shard * (j + 1)])
-        ends_in[s, :, place] = ends_out[core, :, place]
-        return [
-            begin(ends_out.at[peer % 2, :, place], ends_in.at[s, :, place], (d, peer))
-            for peer in seq_peers
-        ]
-
-    (r_down[...],) = sum_end(down_rs)
-    ends = finish_cols(768, hidden, sum_end(up_rs)[0])
-    (r_outs[1],) = sum_end(xout_rs)
-    full, half = sum_end(self_rs)
-    ends += finish_cols(384, 384, full) + finish_half(384, half)
-
-    arrive(home_dp)
-    gain_sum = jnp.zeros((1, width), jnp.float32)
-    shift_sum = jnp.zeros((1, width), jnp.float32)
-    for t in range(tile_count):
-        grad = wide(dn_home[block(0, main)]) * route[0][t]
-        rest = wide(dr_home[0]) * route[0][t]
-        for p in range(1, data_count):
-            grad = grad + wide(dn_home[block(p, main)]) * route[p][t]
-            rest = rest + wide(dr_home[p]) * route[p][t]
-        rest = jnp.concatenate([rest[k : k + 1] for k in range(columns)], axis=1)
-        unit, inverse = norm_parts(wide(img[t, 0:main]))
-        gain_sum = gain_sum + column_sum(grad * unit)
-        shift_sum = shift_sum + column_sum(grad)
-        r_igrad[t, 0:main] = low(norm_back(unit, inverse, vector(5), grad))
-        unit, inverse = norm_parts(wide(img[t, main:real_rows]))
-        gain_sum = gain_sum + rest * unit
-        shift_sum = shift_sum + rest
-        r_igrad[t, main:real_rows] = low(norm_back(unit, inverse, vector(5), rest))
-    vv[5:6] = gain_sum
-    vv[6:7] = shift_sum
-
+    grad = wide(dn[block(s, inbox)])
+    vv[5:6] = column_sum(grad * wide(m.units[...]))
+    vv[6:7] = column_sum(grad)
+    rest = wide(dr_out[s])
+    for row, total in ((5, rest * wide(rest_in[s])), (6, rest)):
+        total = jnp.sum(total, axis=0)
+        total = jnp.concatenate([total[k : k + 1] for k in range(columns)], axis=1)
+        vv[row : row + 1] = vv[row : row + 1] + total
+    first_grad = seq_sum_end(state)
+    unit, inverse = norm_parts(wide(text[0]))
+    vv[1:2] = column_sum(first_grad * unit)
+    vv[2:3] = column_sum(first_grad)
+    r_tgrad[...] = low(dx[...] + norm_back(unit, inverse, vector(1), first_grad))
     vv_out, vv_in, vq = m.vv_out, m.vv_in, m.vq
     everything = vv[...]
     for p in range(data_count):
@@ -1545,11 +1507,9 @@
         peer = (d + k) % data_count
         vv_dp.append(begin(vv_out.at[peer], vv_in.at[d], (peer, s)))
     vv_in[d] = vv_out[d]
-
-    full, half = sum_end(cross_rs)
-    ends += finish_cols(0, 384, full) + finish_half(0, half)
-    (r_outs[0],) = sum_end(sout_rs)
-
+    sum_step(cross_rs, 2)
+    sum_step(cross_rs, 3)
+    sum_middle(sout_rs)
     arrive(vv_dp)
     total = vv_in[0]
     for p in range(1, data_count):
@@ -1557,6 +1517,53 @@
     vq[s] = total
     vq_seq = [begin(vq.at[s], vq.at[s], (d, peer)) for peer in seq_peers]
     bias_grad = total[9:10]
+    r_text[...] = low(x3[...] + seq_sum_end(out_state) + vector(0))
+
+    cols_out, cols_in, ends_out, ends_in = m.cols_out, m.cols_in, m.ends_out, m.ends_in
+
+    def finish_cols(first, size, total):
+        place = lanes(first, size)
+        for j in range(seq_count):
+            cols_out[j, :, place] = low(total[shard * j : shard * (j + 1)])
+        cols_in[s, :, place] = cols_out[s, :, place]
+        return [
+            begin(cols_out.at[peer, :, place], cols_in.at[s, :, place], (d, peer))
+            for peer in seq_peers
+        ]
+
+    def finish_half(first, total):
+        place = lanes(first, 384)
+        for j in range(2):
+            ends_out[j, :, place] = low(total[shard * j : shard * (j + 1)])
+        ends_in[s, :, place] = ends_out[core, :, place]
+        return [
+            begin(ends_out.at[peer % 2, :, place], ends_in.at[s, :, place], (d, peer))
+            for peer in seq_peers
+        ]
+
+    (r_down[...],) = sum_end(down_rs)
+    ends = finish_cols(768, hidden, sum_end(up_rs)[0])
+    (r_outs[1],) = sum_end(xout_rs)
+    full, half = sum_end(self_rs)
+    ends += finish_cols(384, 384, full) + finish_half(384, half)
+
+    arrive(home_dp)
+    for t in range(tile_count):
+        grad = wide(dn_home[block(0, main)]) * route[0][t]
+        rest = wide(dr_home[0]) * route[0][t]
+        for p in range(1, data_count):
+            grad = grad + wide(dn_home[block(p, main)]) * route[p][t]
+            rest = rest + wide(dr_home[p]) * route[p][t]
+        rest = jnp.concatenate([rest[k : k + 1] for k in range(columns)], axis=1)
+        unit, inverse = norm_parts(wide(img[t, 0:main]))
+        r_igrad[t, 0:main] = low(norm_back(unit, inverse, vector(5), grad))
+        unit, inverse = norm_parts(wide(img[t, main:real_rows]))
+        r_igrad[t, main:real_rows] = low(norm_back(unit, inverse, vector(5), rest))
+
+
+    full, half = sum_end(cross_rs)
+    ends += finish_cols(0, 384, full) + finish_half(0, half)
+    (r_outs[0],) = sum_end(sout_rs)
 
     arrive(ends)
     r_cols[...] = cols_in[...]

time: 178 us -> 176 us (0.989)
  Pallas kernels: 174 us -> 171 us
    pallas_call x1, Pallas kernels: 171 us -> 169 us  [fused_device(): pl.pallas_call(partial(fused_kernel, names, len(inputs)), out_shape=packe...]
where the time goes in v3:
time: 176 us; the launch traced here: 175 us
  Pallas kernels  171 us (97%)
  local copies, waits for them, and re-layouts  3.53 us (2%)
    pallas_call x1, Pallas kernels, fused_device(): pl.pallas_call(partial(fused_kernel, names, len(inputs)), out_shape=packe...  169 us

profile of v3, /device:TPU:0, one launch (start us, length us, event | category | flops | bytes accessed | tf_op | source)
XLA Modules:
  0.0 175.5 jit_solution(17344208542995728097)
XLA Ops:
  0.7 1.7 copy.48.refs_3_
  2.4 168.5 %decoder_layer.1 = (bf16[64,768]{1,0:T(8,128)(2,1)}, bf16[64,768]{1,0:T(8,128)(2,1)}, bf16[4,49,768]{2,1,0:T(8,128)(2,1)}, bf16[4,24,1536]{2,1,0:T(8,128)(2,1)},...) custom-call(s32[32]{0:T(128)} %refs_0_.1, s32[8]{0:T(128)} %refs_1_.1, ...), custom_call_target="tpu_custom_call" | custom-call | tf_op jit(solution)/shard_map/decoder_layer/pallas_call | solution.py:1652
  170.9 2.7 %unpack.1 = (bf16[1,64,768]{2,1,0:T(8,128)(2,1)}, bf16[1,64,768]{2,1,0:T(8,128)(2,1)}, bf16[4,49,768]{2,1,0:T(8,128)(2,1)}, f32[24,768]{1,0:T(8,128)}, f32[24,76...) custom-call(bf16[64,768]{1,0:T(8,128)(2,1)} %get-tuple-element.31.t_, ...), custom_call_target="tpu_custom_call" | custom-call | tf_op jit(solution)/shard_map/unpack/pallas_call | solution.py:1675
  173.6 1.8 %copy.49 = bf16[4,49,768]{2,0,1:T(4,128)(2,1)} copy(bf16[4,49,768]{2,1,0:T(8,128)(2,1)} %get-tuple-element.41) | data formatting | bytes 602112 | tf_op jit(solution)/shard_map/unpack/pallas_call | solution.py:1675

commit v4 on v3

--- a/solution.py
+++ b/solution.py
@@ -1429,13 +1429,11 @@
         [m.y_full.at[:, :, lanes(384, 384)], m.y_half.at[:, :, lanes(384, 384)]],
         [m.z_full.at[:, :, lanes(384, 384)], m.z_half.at[:, :, lanes(384, 384)]],
     )
-    out_state = seq_sum_begin(3, lambda i, j: dot_plain(pick(act, i, j), down_all[...]))
     tile_grads(block(sibling, inbox))
     pair_own = begin(dn.at[block(sibling, inbox)], dn_pair.at[0], (d, sibling))
     tile_grads(block(s, inbox))
 
     sum_middle(xout_rs)
-    out_state = seq_sum_pass(out_state)
     grad = dot_left(h2[...], dq2[...])
     g_cols[:, 0:128] = low(grad[:, 0:128])
     g_half[:, :, :, 0:128] = low(grad[:, 128:256]).reshape(*half_shape, 128)
@@ -1454,9 +1452,6 @@
         [m.z_full.at[:, :, lanes(0, 384)], m.z_half.at[:, :, lanes(0, 384)]],
     )
     sum_step(self_rs, 1)
-    arrive(sout_seq)
-    sout_view = lambda index: [g_out.at[index, :, lanes(0, width)]]
-    sout_rs = sum_begin(sout_view, [m.y_sout], [m.z_sout])
     arrive([pair_own, rest_far])
     dr_out[s] = low(wide(dr_out[s]) + wide(dr_pair[0]) + wide(dr_far[...]))
 
@@ -1484,6 +1479,7 @@
         home_send(k)
     dn_home[own_home] = dn[block(s * data_count + d, main)]
     dr_home[d] = dr_out[s, d]
+    out_state = seq_sum_begin(3, lambda i, j: dot_plain(pick(act, i, j), down_all[...]))
     grad = wide(dn[block(s, inbox)])
     vv[5:6] = column_sum(grad * wide(m.units[...]))
     vv[6:7] = column_sum(grad)
@@ -1507,6 +1503,10 @@
         peer = (d + k) % data_count
         vv_dp.append(begin(vv_out.at[peer], vv_in.at[d], (peer, s)))
     vv_in[d] = vv_out[d]
+    arrive(sout_seq)
+    sout_view = lambda index: [g_out.at[index, :, lanes(0, width)]]
+    sout_rs = sum_begin(sout_view, [m.y_sout], [m.z_sout])
+    out_state = seq_sum_pass(out_state)
     sum_step(cross_rs, 2)
     sum_step(cross_rs, 3)
     sum_middle(sout_rs)

time: 176 us -> 170 us (0.966)
  Pallas kernels: 171 us -> 164 us
    pallas_call x1, Pallas kernels: 169 us -> 161 us  [fused_device(): pl.pallas_call(partial(fused_kernel, names, len(inputs)), out_shape=packe...]
where the time goes in v4:
time: 170 us; the launch traced here: 168 us
  Pallas kernels  164 us (96%)
  local copies, waits for them, and re-layouts  3.53 us (2%)
    pallas_call x1, Pallas kernels, fused_device(): pl.pallas_call(partial(fused_kernel, names, len(inputs)), out_shape=packe...  161 us

profile of v4, /device:TPU:0, one launch (start us, length us, event | category | flops | bytes accessed | tf_op | source)
XLA Modules:
  0.0 168.3 jit_solution(1798662652290021337)
XLA Ops:
  0.7 1.7 %copy.48.refs_3_ = bf16[4,49,768]{2,1,0:T(8,128)(2,1)} copy(bf16[4,49,768]{2,0,1:T(4,128)(2,1)} %param.26) | data formatting | bytes 602112 | tf_op args[1]
  2.4 161.4 %decoder_layer.1 = (bf16[64,768]{1,0:T(8,128)(2,1)}, bf16[64,768]{1,0:T(8,128)(2,1)}, bf16[4,49,768]{2,1,0:T(8,128)(2,1)}, bf16[4,24,1536]{2,1,0:T(8,128)(2,1)},...) custom-call(s32[32]{0:T(128)} %refs_0_.1, s32[8]{0:T(128)} %refs_1_.1, ...), custom_call_target="tpu_custom_call" | custom-call | tf_op jit(solution)/shard_map/decoder_layer/pallas_call | solution.py:1652
  163.8 2.7 %unpack.1 = (bf16[1,64,768]{2,1,0:T(8,128)(2,1)}, bf16[1,64,768]{2,1,0:T(8,128)(2,1)}, bf16[4,49,768]{2,1,0:T(8,128)(2,1)}, f32[24,768]{1,0:T(8,128)}, f32[24,76...) custom-call(bf16[64,768]{1,0:T(8,128)(2,1)} %get-tuple-element.31.t_, ...), custom_call_target="tpu_custom_call" | custom-call | tf_op jit(solution)/shard_map/unpack/pallas_call | solution.py:1675
  166.5 1.8 %copy.49 = bf16[4,49,768]{2,0,1:T(4,128)(2,1)} copy(bf16[4,49,768]{2,1,0:T(8,128)(2,1)} %get-tuple-element.41) | data formatting | bytes 602112 | tf_op jit(solution)/shard_map/unpack/pallas_call | solution.py:1675

commit v5 on v4

--- a/solution.py
+++ b/solution.py
@@ -1507,6 +1507,31 @@
     sout_view = lambda index: [g_out.at[index, :, lanes(0, width)]]
     sout_rs = sum_begin(sout_view, [m.y_sout], [m.z_sout])
     out_state = seq_sum_pass(out_state)
+    cols_out, cols_in, ends_out, ends_in = m.cols_out, m.cols_in, m.ends_out, m.ends_in
+
+    def finish_cols(first, size, total):
+        place = lanes(first, size)
+        for j in range(seq_count):
+            cols_out[j, :, place] = low(total[shard * j : shard * (j + 1)])
+        cols_in[s, :, place] = cols_out[s, :, place]
+        return [
+            begin(cols_out.at[peer, :, place], cols_in.at[s, :, place], (d, peer))
+            for peer in seq_peers
+        ]
+
+    def finish_half(first, total):
+        place = lanes(first, 384)
+        for j in range(2):
+            ends_out[j, :, place] = low(total[shard * j : shard * (j + 1)])
+        ends_in[s, :, place] = ends_out[core, :, place]
+        return [
+            begin(ends_out.at[peer % 2, :, place], ends_in.at[s, :, place], (d, peer))
+            for peer in seq_peers
+        ]
+
+    (r_down[...],) = sum_end(down_rs)
+    ends = finish_cols(768, hidden, sum_end(up_rs)[0])
+    (r_outs[1],) = sum_end(xout_rs)
     sum_step(cross_rs, 2)
     sum_step(cross_rs, 3)
     sum_middle(sout_rs)
@@ -1519,31 +1544,6 @@
     bias_grad = total[9:10]
     r_text[...] = low(x3[...] + seq_sum_end(out_state) + vector(0))
 
-    cols_out, cols_in, ends_out, ends_in = m.cols_out, m.cols_in, m.ends_out, m.ends_in
-
-    def finish_cols(first, size, total):
-        place = lanes(first, size)
-        for j in range(seq_count):
-            cols_out[j, :, place] = low(total[shard * j : shard * (j + 1)])
-        cols_in[s, :, place] = cols_out[s, :, place]
-        return [
-            begin(cols_out.at[peer, :, place], cols_in.at[s, :, place], (d, peer))
-            for peer in seq_peers
-        ]
-
-    def finish_half(first, total):
-        place = lanes(first, 384)
-        for j in range(2):
-            ends_out[j, :, place] = low(total[shard * j : shard * (j + 1)])
-        ends_in[s, :, place] = ends_out[core, :, place]
-        return [
-            begin(ends_out.at[peer % 2, :, place], ends_in.at[s, :, place], (d, peer))
-            for peer in seq_peers
-        ]
-
-    (r_down[...],) = sum_end(down_rs)
-    ends = finish_cols(768, hidden, sum_end(up_rs)[0])
-    (r_outs[1],) = sum_end(xout_rs)
     full, half = sum_end(self_rs)
     ends += finish_cols(384, 384, full) + finish_half(384, half)
 

time: 170 us -> 169 us (level)
  no operation moved by 1% of the time
where the time goes in v5:
time: 169 us; the launch traced here: 168 us
  Pallas kernels  164 us (97%)
  local copies, waits for them, and re-layouts  3.53 us (2%)
    pallas_call x1, Pallas kernels, fused_device(): pl.pallas_call(partial(fused_kernel, names, len(inputs)), out_shape=packe...  161 us

profile of v5, /device:TPU:0, one launch (start us, length us, event | category | flops | bytes accessed | tf_op | source)
XLA Modules:
  0.0 168.3 jit_solution(4907829753069673713)
XLA Ops:
  0.7 1.7 %copy.48.refs_3_ = bf16[4,49,768]{2,1,0:T(8,128)(2,1)} copy(bf16[4,49,768]{2,0,1:T(4,128)(2,1)} %param.26) | data formatting | bytes 602112 | tf_op args[1]
  2.4 161.4 %decoder_layer.1 = (bf16[64,768]{1,0:T(8,128)(2,1)}, bf16[64,768]{1,0:T(8,128)(2,1)}, bf16[4,49,768]{2,1,0:T(8,128)(2,1)}, bf16[4,24,1536]{2,1,0:T(8,128)(2,1)},...) custom-call(s32[32]{0:T(128)} %refs_0_.1, s32[8]{0:T(128)} %refs_1_.1, ...), custom_call_target="tpu_custom_call" | custom-call | tf_op jit(solution)/shard_map/decoder_layer/pallas_call | solution.py:1652
  163.8 2.7 %unpack.1 = (bf16[1,64,768]{2,1,0:T(8,128)(2,1)}, bf16[1,64,768]{2,1,0:T(8,128)(2,1)}, bf16[4,49,768]{2,1,0:T(8,128)(2,1)}, f32[24,768]{1,0:T(8,128)}, f32[24,76...) custom-call(bf16[64,768]{1,0:T(8,128)(2,1)} %get-tuple-element.31.t_, ...), custom_call_target="tpu_custom_call" | custom-call | tf_op jit(solution)/shard_map/unpack/pallas_call | solution.py:1675
  166.5 1.8 %copy.49 = bf16[4,49,768]{2,0,1:T(4,128)(2,1)} copy(bf16[4,49,768]{2,1,0:T(8,128)(2,1)} %get-tuple-element.41) | data formatting | bytes 602112 | tf_op jit(solution)/shard_map/unpack/pallas_call | solution.py:1675
